TPU v7x, 32 devices: a whole 2x2x4 slice. The times are simulated.
32 devices in a mesh: dp: 4 (over z), seq: 8 (over y, x, core).
Axes of the slice: x: 2, y: 2, z: 4, core: 2. Of those that a mesh axis runs over, the one named last changes fastest.
Arguments:
- tokens: bfloat16 [4, 3072, 4096], P('dp', 'seq'), may hold values from -16 to 16
- qkv_weight: bfloat16 [4096, 3072], P(('dp', 'seq')), may hold values from -1 to 1
- segments: int32 [4, 3072], P('dp', 'seq'), may hold values from 0 to 3071, as said below
- destination: int32 [4, 3072], P('dp', 'seq'), may hold values from 0 to 3071, as said below
- doc_prefix: int32 [4, 8], P('dp', 'seq'), may hold values from 0 to 768, as said below
Outputs:
- attended: bfloat16 [4, 3072, 2048], P('dp', 'seq')
Inputs may be any that keep to these rules, and one draw needn't show every extreme that they name: `segments`: A token's id is the position in its sequence of its document's first token, so ids never fall and start at 0; the last token of every sequence is a document of its own. doc_prefix[b, d] is the number of tokens before row d * 384 of sequence b with that row's segment id; the most is reached in every draw. `destination`: each row is a permutation; the tokens of one device go to exactly 8 devices of the sequence, exactly 48 to each, and every device receives tokens from exactly 8 devices.
All inputs are finite; a program needn't handle non-finite values.
Results may differ from a plain program's by a relative error of at most 0.012.
The roundings to bfloat16 on the way count: a program that leaves them out, or rounds other values in their place, can miss the bound.
Values may be sent and summed in bfloat16 or wider, within the bound.
A program may use at most 128 MiB of HBM per device.

v0:
```python
import jax
import jax.numpy as jnp
from jax import lax
from jax.sharding import PartitionSpec as P

HEADS = 16
KV_HEADS = 4
HEAD_DIM = 128
REACH = 2


ROPE_BASE = 500000.0
MASKED = -1e30


def shifted(block, axis, distance):
    devices = range(lax.axis_size(axis))
    route = [(i - distance, i) for i in devices if i - distance in devices]
    return lax.ppermute(block, axis, route)


def positions(segment_ids, prefix_len):
    index_list = jnp.arange(segment_ids.shape[0], dtype=jnp.int32)
    fresh_doc = jnp.concatenate([jnp.ones((1,), jnp.bool_), segment_ids[1:] != segment_ids[:-1]])
    first_row = lax.cummax(jnp.where(fresh_doc, index_list, 0), axis=0)
    leading = segment_ids == segment_ids[0]
    position = index_list - first_row + jnp.where(leading, prefix_len, 0)
    return (position, leading)


def rotate(heads, position):
    half_dim = heads.shape[-1] // 2
    frequency = ROPE_BASE ** (-2.0 * jnp.arange(half_dim, dtype=jnp.float32) / heads.shape[-1])
    angles = position.astype(jnp.float32)[:, None] * frequency[None, :]
    cosine = jnp.cos(angles)[:, None, :]
    sine = jnp.sin(angles)[:, None, :]
    first_half = heads[..., :half_dim]
    second_half = heads[..., half_dim:]
    return jnp.concatenate(
        [first_half * cosine - second_half * sine, second_half * cosine + first_half * sine],
        axis=-1,
    )


def visible_keys(segment_ids, leading, prefix_len, reach):
    count = segment_ids.shape[0]
    query_rows = jnp.arange(count, dtype=jnp.int32)
    columns = jnp.arange((reach + 1) * count, dtype=jnp.int32) - reach * count
    key_segments = jnp.concatenate([jnp.full((reach * count,), -1, jnp.int32), segment_ids])
    local_part = (
        (columns[None, :] >= 0)
        & (columns[None, :] <= query_rows[:, None])
        & (key_segments[None, :] == segment_ids[:, None])
    )
    remote_part = (columns[None, :] < 0) & (columns[None, :] >= -prefix_len) & leading[:, None]
    return local_part | remote_part


def on_device(tokens, qkv_weight, segments, destination, doc_prefix):
    token_rows = tokens[0]
    segment_ids = segments[0]
    targets = destination[0]
    prefix_len = doc_prefix[0, 0]
    tok_count = token_rows.shape[0]
    query_width = HEADS * HEAD_DIM
    kv_width = KV_HEADS * HEAD_DIM
    group_size = HEADS // KV_HEADS
    projected = jnp.dot(
        token_rows,
        lax.all_gather(qkv_weight, ("dp", "seq"), axis=0, tiled=True),
        preferred_element_type=jnp.float32,
    )
    position, leading = positions(segment_ids, prefix_len)
    queries = rotate(
        projected[:, :query_width].reshape(tok_count, HEADS, HEAD_DIM), position
    ).astype(jnp.bfloat16)
    keys_rot = rotate(
        projected[:, query_width : query_width + kv_width].reshape(tok_count, KV_HEADS, HEAD_DIM),
        position,
    ).astype(jnp.bfloat16)
    values = projected[:, query_width + kv_width :].astype(jnp.bfloat16)
    kv_block = jnp.concatenate([keys_rot.reshape(tok_count, kv_width), values], axis=1)
    pieces = []
    moving = kv_block
    for hop_index in range(REACH):
        moving = shifted(moving, "seq", 1)
        pieces.append(moving)
    window = jnp.concatenate(pieces[::-1] + [kv_block], axis=0)
    key_len = window.shape[0]
    key_heads = window[:, :kv_width].reshape(key_len, KV_HEADS, HEAD_DIM).transpose(1, 0, 2)
    value_heads = window[:, kv_width:].reshape(key_len, KV_HEADS, HEAD_DIM).transpose(1, 0, 2)
    query_heads = queries.reshape(tok_count, KV_HEADS, group_size, HEAD_DIM).transpose(1, 0, 2, 3)
    key_mask = visible_keys(segment_ids, leading, prefix_len, REACH)

    def head_block(operands):
        query_part, key_part, value_part = operands
        scores = jnp.einsum(
            "tgd,ld->gtl", query_part, key_part, preferred_element_type=jnp.float32
        ) * HEAD_DIM ** (-0.5)
        scores = jnp.where(key_mask[None], scores, MASKED)
        top_score = jnp.max(scores, axis=-1, keepdims=True)
        expo = jnp.exp(scores - top_score)
        row_total = jnp.sum(expo, axis=-1, keepdims=True)
        probs = (expo / row_total).astype(jnp.bfloat16)
        return jnp.einsum(
            "gtl,ld->tgd", probs, value_part, preferred_element_type=jnp.float32
        ).astype(jnp.bfloat16)

    head_outs = lax.map(head_block, (query_heads, key_heads, value_heads))
    heads_out = head_outs.transpose(1, 0, 2, 3).reshape(tok_count, query_width)
    seq_count = lax.axis_size("seq")
    capacity = tok_count // min(seq_count, 16)
    owner_dev = targets // tok_count
    place_row = targets % tok_count
    one_hot = (owner_dev[:, None] == jnp.arange(seq_count, dtype=jnp.int32)[None, :]).astype(
        jnp.int32
    )
    slot_rank = jnp.sum(jnp.cumsum(one_hot, axis=0) * one_hot, axis=1) - 1
    slot_index = owner_dev * capacity + slot_rank
    send_rows = (
        jnp.zeros((seq_count * capacity, query_width), jnp.bfloat16).at[slot_index].set(heads_out)
    )
    send_places = (
        jnp.full((seq_count * capacity,), tok_count, jnp.int32).at[slot_index].set(place_row)
    )
    got_rows, got_places = (
        lax.all_to_all(send_rows, "seq", split_axis=0, concat_axis=0, tiled=True),
        lax.all_to_all(send_places, "seq", split_axis=0, concat_axis=0, tiled=True),
    )
    result = (
        jnp.zeros((tok_count, query_width), jnp.bfloat16).at[got_places].set(got_rows, mode="drop")
    )
    return result[None]


def solution(mesh):
    placed = (
        P("dp", "seq", None),
        P(("dp", "seq"), None),
        P("dp", "seq"),
        P("dp", "seq"),
        P("dp", "seq"),
    )
    return jax.shard_map(
        on_device, mesh=mesh, in_specs=placed, out_specs=P("dp", "seq", None), check_vma=False
    )
```

profile of v0, /device:TPU:0, one launch (start us, length us, event | category | flops | bytes accessed | tf_op | source)
XLA Modules:
  0.0 298.0 jit_solution(17385272415409930039)
XLA Ops:
  6.5 0.7 all-gather.2.cloned.1.call-update
  8.1 1.2 slice.61
  9.3 0.7 reduce.11
  10.0 0.8 compare_reduce_fusion
  10.8 0.1 add_select_fusion.3
  10.9 0.3 reduce-window.19
  11.2 0.1 slice.59
  11.3 0.7 compare_reduce_fusion.1
  12.1 0.7 fusion.75
  12.8 0.9 reduce-window.15
  13.7 0.1 slice_reduce_fusion.1
  13.8 0.7 fusion.67
  14.5 1.6 multiply_cosine_fusion
  16.1 151.5 %all-gather.2.cloned.1.call-done = bf16[4096,3072]{1,0:T(8,128)(2,1)} async-done(((bf16[128,3072]{1,0:T(8,128)(2,1)}), bf16[4096,3072]{1,0:T(8,128)(2,1)}) %all-gather.2.cloned.1.call-update) | async-done | bytes 25165840 | tf_op jit(solution)/shard_map/all_gather | solution.py:70
  167.6 13.4 %fusion.54 = f32[384,3072]{1,0:T(8,128)S(1)} fusion(bf16[4096,3072]{1,0:T(8,128)(2,1)} %all-gather.2.cloned.1.call-done, bf16[1,384,4096]{2,1,0:T(8,128)(2,1)S(1)} %copy-done), kind=kOutput, calls=%fused_computation.41 | convolution fusion | flops 9663676416 | bytes 33030144 | tf_op jit(solution)/shard_map/dot_general | solution.py:68
  181.1 2.1 copy-done.3
  183.2 0.3 reshape.293
  183.5 0.6 copy-done.6
  184.1 0.1 copy-done.8
  184.2 0.6 subtract_convert_fusion.1
  184.8 0.5 pad_maximum_fusion.1
  185.4 0.1 copy.33
  185.4 0.1 pad_maximum_fusion
  185.5 2.2 collective-permute-start
  187.8 0.2 slice_reduce_fusion
  188.0 0.1 fusion.60
  188.2 2.9 scatter_custom_fusion
  191.1 0.7 all_to_all.16
  191.8 3.6 %all-to-all-start = ((s32[8,48,1]{1,2,0:T(1,128)}), s32[8,48,1]{1,2,0:T(1,128)S(1)}, u32[]{:S(2)}, u32[]{:S(2)}) async-start(s32[8,48,1]{1,2,0:T(1,128)} %all_to_all.16), calls=%async_computation | async-start | bytes 8192 | tf_op jit(solution)/shard_map/all_to_all | solution.py:128
  195.5 4.4 %collective-permute-start.1 = (bf16[384,1024]{1,0:T(8,128)(2,1)S(1)}, bf16[384,1024]{1,0:T(8,128)(2,1)S(1)}, u32[]{:S(2)}, u32[]{:S(2)}) collective-permute-start(bf16[384,1024]{1,0:T(8,128)(2,1)S(1)} %collective-permute-done), channel_id=1, source_target_pairs={{0,1},{1,2},{2,3},{3,4},{4,5},{5,6},{6,7},{8,9},{9,10},{10,11},{11... | collective-permute-start | bytes 2359304 | tf_op jit(solution)/shard_map/ppermute | solution.py:19
  199.9 2.1 slice_bitcast_fusion
  202.0 0.7 copy.29
  202.7 0.2 copy-done.7
  202.9 0.1 copy-done.9
  203.0 1.3 subtract_convert_fusion
  204.3 0.4 copy.21
  204.7 0.4 copy.22
  205.1 2.0 maximum_bitcast_fusion
  207.2 0.2 maximum_maximum_fusion
  207.4 1.3 slice_bitcast_fusion.1
  208.7 1.2 copy.32
  209.9 0.4 copy-done.2
  210.3 1.4 copy.25
  211.7 38.6 %while.11 = (s32[]{:T(128)}, bf16[4,384,4,128]{1,3,2,0:T(8,128)(2,1)S(1)}, bf16[4,1152,128]{1,2,0:T(8,128)(2,1)}, bf16[4,1152,128]{2,1,0:T(8,128)(2,1)}, bf16[4,...) while((s32[]{:T(128)}, ...), condition=%wide.region_9.10_spmd.clone, body=%wide.region_6.9_spmd.clone.sunk | while | flops 1377734400 | bytes 3420413 | solution.py:109
  211.7 1.3 fusion.95
  213.0 3.7 %fusion.96 = f32[4,384]{1,0:T(4,128)S(1)} fusion(pred[384,1152]{0,1:T(8,128)(4,1)S(1)} %fusion.95, bf16[4,384,4,128]{3,1,2,0:T(8,128)(2,1)} %get-tuple-element.204, s32[]{:T(128)S(6)} %copy.37, bf16[4,1152,128]{2,1,0:T(8,128)(2,1)} %get-tuple-element.203), kind=kOutput, calls=%fused_computation.101.clone.1 | convolution fusion | flops 460063872 | bytes 1137664 | tf_op jit(solution)/shard_map/while/body/eval_jaxpr/sub | solution.py:102
  216.7 4.6 %fusion.97 = bf16[4,384,4,128]{1,3,2,0:T(8,128)(2,1)S(1)} fusion(bf16[4,384,4,128]{1,3,2,0:T(8,128)(2,1)S(1)} %get-tuple-element.189, s32[]{:T(128)S(6)} %copy.37, f32[4,384]{1,0:T(4,128)S(1)} %fusion.96, bf16[4,1152,128]{1,2,0:T(8,128)(2,1)} %get-tuple-element.202, pred[384,1152]{0,1:T(8,128)(4,1)S(1)} %fusion.95, ...), kind=kOutput, calls=%fused_computation.20.clone.1 | convolution fusion | flops 915016320 | bytes 1826816 | tf_op jit(solution)/shard_map/while/body/eval_jaxpr/gtl,ld->tgd/dot_general | solution.py:105
  221.4 1.3 fusion.95
  222.7 3.7 %fusion.96 = f32[4,384]{1,0:T(4,128)S(1)} fusion(pred[384,1152]{0,1:T(8,128)(4,1)S(1)} %fusion.95, bf16[4,384,4,128]{3,1,2,0:T(8,128)(2,1)} %get-tuple-element.204, s32[]{:T(128)S(6)} %copy.37, bf16[4,1152,128]{2,1,0:T(8,128)(2,1)} %get-tuple-element.203), kind=kOutput, calls=%fused_computation.101.clone.1 | convolution fusion | flops 460063872 | bytes 1137664 | tf_op jit(solution)/shard_map/while/body/eval_jaxpr/sub | solution.py:102
  226.3 4.6 %fusion.97 = bf16[4,384,4,128]{1,3,2,0:T(8,128)(2,1)S(1)} fusion(bf16[4,384,4,128]{1,3,2,0:T(8,128)(2,1)S(1)} %get-tuple-element.189, s32[]{:T(128)S(6)} %copy.37, f32[4,384]{1,0:T(4,128)S(1)} %fusion.96, bf16[4,1152,128]{1,2,0:T(8,128)(2,1)} %get-tuple-element.202, pred[384,1152]{0,1:T(8,128)(4,1)S(1)} %fusion.95, ...), kind=kOutput, calls=%fused_computation.20.clone.1 | convolution fusion | flops 915016320 | bytes 1826816 | tf_op jit(solution)/shard_map/while/body/eval_jaxpr/gtl,ld->tgd/dot_general | solution.py:105
  231.0 1.3 fusion.95
  232.3 3.7 %fusion.96 = f32[4,384]{1,0:T(4,128)S(1)} fusion(pred[384,1152]{0,1:T(8,128)(4,1)S(1)} %fusion.95, bf16[4,384,4,128]{3,1,2,0:T(8,128)(2,1)} %get-tuple-element.204, s32[]{:T(128)S(6)} %copy.37, bf16[4,1152,128]{2,1,0:T(8,128)(2,1)} %get-tuple-element.203), kind=kOutput, calls=%fused_computation.101.clone.1 | convolution fusion | flops 460063872 | bytes 1137664 | tf_op jit(solution)/shard_map/while/body/eval_jaxpr/sub | solution.py:102
  236.0 4.6 %fusion.97 = bf16[4,384,4,128]{1,3,2,0:T(8,128)(2,1)S(1)} fusion(bf16[4,384,4,128]{1,3,2,0:T(8,128)(2,1)S(1)} %get-tuple-element.189, s32[]{:T(128)S(6)} %copy.37, f32[4,384]{1,0:T(4,128)S(1)} %fusion.96, bf16[4,1152,128]{1,2,0:T(8,128)(2,1)} %get-tuple-element.202, pred[384,1152]{0,1:T(8,128)(4,1)S(1)} %fusion.95, ...), kind=kOutput, calls=%fused_computation.20.clone.1 | convolution fusion | flops 915016320 | bytes 1826816 | tf_op jit(solution)/shard_map/while/body/eval_jaxpr/gtl,ld->tgd/dot_general | solution.py:105
  240.7 1.3 fusion.95
  242.0 3.7 %fusion.96 = f32[4,384]{1,0:T(4,128)S(1)} fusion(pred[384,1152]{0,1:T(8,128)(4,1)S(1)} %fusion.95, bf16[4,384,4,128]{3,1,2,0:T(8,128)(2,1)} %get-tuple-element.204, s32[]{:T(128)S(6)} %copy.37, bf16[4,1152,128]{2,1,0:T(8,128)(2,1)} %get-tuple-element.203), kind=kOutput, calls=%fused_computation.101.clone.1 | convolution fusion | flops 460063872 | bytes 1137664 | tf_op jit(solution)/shard_map/while/body/eval_jaxpr/sub | solution.py:102
  245.6 4.6 %fusion.97 = bf16[4,384,4,128]{1,3,2,0:T(8,128)(2,1)S(1)} fusion(bf16[4,384,4,128]{1,3,2,0:T(8,128)(2,1)S(1)} %get-tuple-element.189, s32[]{:T(128)S(6)} %copy.37, f32[4,384]{1,0:T(4,128)S(1)} %fusion.96, bf16[4,1152,128]{1,2,0:T(8,128)(2,1)} %get-tuple-element.202, pred[384,1152]{0,1:T(8,128)(4,1)S(1)} %fusion.95, ...), kind=kOutput, calls=%fused_computation.20.clone.1 | convolution fusion | flops 915016320 | bytes 1826816 | tf_op jit(solution)/shard_map/while/body/eval_jaxpr/gtl,ld->tgd/dot_general | solution.py:105
  250.3 0.8 copy.26
  251.1 4.1 %scatter_custom_fusion.1 = bf16[384,2048]{1,0:T(8,128)(2,1)} fusion(s32[384]{0:T(512)S(1)} %fusion.68, bf16[384,2048]{1,0:T(8,128)(2,1)S(1)} %copy.26, bf16[]{:T(256)} %constant.45.clone.1), kind=kCustom, calls=%fused_computation.55 | custom fusion | bytes 1572866 | tf_op jit(solution)/shard_map/scatter | solution.py:121
  255.2 9.9 %all-to-all-start.1 = ((bf16[8,48,2048]{2,1,0:T(8,128)(2,1)}), bf16[8,48,2048]{2,1,0:T(8,128)(2,1)}, u32[]{:S(2)}, u32[]{:S(2)}) async-start(bf16[8,48,2048]{2,1,0:T(8,128)(2,1)} %bitcast.138), calls=%async_computation.1 | async-start | bytes 3145728 | tf_op jit(solution)/shard_map/all_to_all | solution.py:127
  265.0 0.5 broadcast.329
  265.6 0.6 reduce.22
  266.2 0.1 all_to_all.18
  266.3 19.9 %all-to-all-done.1 = bf16[8,48,2048]{2,1,0:T(8,128)(2,1)} async-done(((bf16[8,48,2048]{2,1,0:T(8,128)(2,1)}), bf16[8,48,2048]{2,1,0:T(8,128)(2,1)}, u32[]{:S(2)}, u32[]{:S(2)}) %all-to-all-start.1) | async-done | bytes 1572896 | tf_op jit(solution)/shard_map/all_to_all | solution.py:127
  286.2 5.0 %scatter_custom_fusion.2 = bf16[384,2048]{1,0:T(8,128)(2,1)} fusion(s32[384]{0:T(512)S(1)} %fusion.69, bf16[384,2048]{1,0:T(8,128)(2,1)} %bitcast.18, bf16[]{:T(256)} %constant.45.clone.1), kind=kCustom, calls=%fused_computation.53 | custom fusion | bytes 1573376 | tf_op jit(solution)/shard_map/scatter | solution.py:131
  (37 shorter events, 0.3 us)
Async XLA Ops:
  6.5 161.1 %copy-start = (bf16[1,384,4096]{2,1,0:T(8,128)(2,1)S(1)}, bf16[1,384,4096]{2,1,0:T(8,128)(2,1)}, u32[]{:S(2)}) copy-start(bf16[1,384,4096]{2,1,0:T(8,128)(2,1)} %param.7) | copy-start | bytes 9437188
  6.5 161.1 %all-gather.2.cloned.1.call-start = ((), (), s32[]{:S(2)}) async-start(), calls=%async_computation.2 | async-start | bytes 25952256 | tf_op jit(solution)/shard_map/all_gather | solution.py:70
  181.0 2.1 copy-start.3
  183.2 0.9 copy-start.6
  183.2 1.0 copy-start.8
  184.8 3.3 %copy-start.11 = (s32[1,384]{1,0:T(1,128)S(1)}, s32[1,384]{1,0:T(1,128)}, u32[]{:S(2)}) copy-start(s32[1,384]{1,0:T(1,128)} %param.10) | copy-start | bytes 4612
  185.4 10.0 %copy-start.4 = (bf16[48,8,4,128]{3,1,2,0:T(8,128)(2,1)}, bf16[48,8,4,128]{3,1,2,0:T(8,128)(2,1)S(1)}, u32[]{:S(2)}) copy-start(bf16[48,8,4,128]{3,1,2,0:T(8,128)(2,1)S(1)} %copy.33) | copy-start | bytes 1179652
  185.5 9.9 %collective-permute-start = (bf16[384,1024]{1,0:T(8,128)(2,1)S(1)}, bf16[384,1024]{1,0:T(8,128)(2,1)S(1)}, u32[]{:S(2)}, u32[]{:S(2)}) collective-permute-start(bf16[384,1024]{1,0:T(8,128)(2,1)S(1)} %pad_maximum_fusion), channel_id=1, source_target_pairs={{0,1},{1,2},{2,3},{3,4},{4,5},{5,6},{6,7},{8,9},{9,10},{10,11},{11... | collective-permute-start | bytes 2359304 | tf_op jit(solution)/shard_map/ppermute | solution.py:19
  191.8 63.4 %all-to-all-start = ((s32[8,48,1]{1,2,0:T(1,128)}), s32[8,48,1]{1,2,0:T(1,128)S(1)}, u32[]{:S(2)}, u32[]{:S(2)}) async-start(s32[8,48,1]{1,2,0:T(1,128)} %all_to_all.16), calls=%async_computation | async-start | bytes 8192 | tf_op jit(solution)/shard_map/all_to_all | solution.py:128
  195.5 11.7 %collective-permute-start.1 = (bf16[384,1024]{1,0:T(8,128)(2,1)S(1)}, bf16[384,1024]{1,0:T(8,128)(2,1)S(1)}, u32[]{:S(2)}, u32[]{:S(2)}) collective-permute-start(bf16[384,1024]{1,0:T(8,128)(2,1)S(1)} %collective-permute-done), channel_id=1, source_target_pairs={{0,1},{1,2},{2,3},{3,4},{4,5},{5,6},{6,7},{8,9},{9,10},{10,11},{11... | collective-permute-start | bytes 2359304 | tf_op jit(solution)/shard_map/ppermute | solution.py:19
  202.0 0.9 copy-start.7
  202.0 1.0 copy-start.9
  205.1 2.0 copy-start.5
  208.7 1.6 copy-start.2
  209.9 1.8 copy-start.10
  255.2 36.0 %copy-start.1 = (bf16[1,384,4096]{2,1,0:T(8,128)(2,1)S(1)}, bf16[1,384,4096]{2,1,0:T(8,128)(2,1)}, u32[]{:S(2)}) copy-start(bf16[1,384,4096]{2,1,0:T(8,128)(2,1)} %param.7) | copy-start | bytes 9437188
  255.2 31.0 %all-to-all-start.1 = ((bf16[8,48,2048]{2,1,0:T(8,128)(2,1)}), bf16[8,48,2048]{2,1,0:T(8,128)(2,1)}, u32[]{:S(2)}, u32[]{:S(2)}) async-start(bf16[8,48,2048]{2,1,0:T(8,128)(2,1)} %bitcast.138), calls=%async_computation.1 | async-start | bytes 3145728 | tf_op jit(solution)/shard_map/all_to_all | solution.py:127
Sparse Core Ops, SparseCore 0:
  10.2 157.3 all-gather.1
where the time goes:
time: 299 us; the launch traced here: 298 us
  waiting for transfers between devices  172 us (58%)
  matrix products  46.7 us (16%)
  local copies, waits for them, and re-layouts  27.1 us (9%)
  starting transfers between devices  20.1 us (7%)
  other arithmetic  17.3 us (6%)
  between operations  14.5 us (5%)
    all_gather x1, waiting for transfers between devices, on_device(): lax.all_gather(qkv_weight, ('dp', 'seq'), axis=0, tiled=True)  152 us
    all_to_all x1, waiting for transfers between devices, on_device(): lax.all_to_all(send_rows, 'seq', split_axis=0, concat_axis=0, tiled=True)  19.9 us
    dot_general x4, matrix products, head_block(): jnp.einsum('gtl,ld->tgd', probs, value_part, preferred_element_type=jnp.f...  18.6 us
    sub x4, matrix products, head_block(): expo = jnp.exp(scores - top_score)  14.7 us
    dot_general x1, matrix products, on_device(): jnp.dot(token_rows, lax.all_gather(qkv_weight, ('dp', 'seq'), axis=0, til...  13.4 us
    all_to_all x1, starting transfers between devices, on_device(): lax.all_to_all(send_rows, 'seq', split_axis=0, concat_axis=0, tiled=True)  9.86 us
    unnamed x28, local copies, waits for them, and re-layouts  7.62 us
    ppermute x2, starting transfers between devices, shifted(): return lax.ppermute(block, axis, route)  6.65 us
  transfers between devices with their start and end apart: 5, of which 2 were waited for; matrix products, arithmetic and copies ran while one was open for 22% of the time, Pallas kernels for 0%

commit v1 on v0

v1 whole, which is shorter than its diff:
```python
import functools

import jax
import jax.numpy as jnp
from jax import lax
from jax.experimental import pallas as pl
from jax.experimental.pallas import tpu as pltpu
from jax.sharding import PartitionSpec as P

HEADS = 16
KV_HEADS = 4
HEAD_DIM = 128
REACH = 2
ROPE_BASE = 500000.0
MASKED = -1e30
CORES = 2
MESH = pl.DeviceIdType.MESH
META_ROWS = 8

ORDERS = ("zyx", "zxy", "xyz")


def part_bounds(width):
    unit = width // 12
    return ((0, 5 * unit), (5 * unit, 4 * unit), (9 * unit, 3 * unit))


def forwards(order, offset, depth):
    delta = dict(zip("xyz", offset))
    last = max([order.index(a) for a in order if delta[a]], default=-1)
    hops = []
    for index, axis in enumerate(order):
        if index < last:
            continue
        if axis == "z":
            steps = (1, -1) if delta["z"] == 0 else ((1,) if delta["z"] < 0 else (-1,))
            for step in steps:
                if abs(delta["z"] - step) < depth:
                    hops.append(("z", step, (delta["x"], delta["y"], delta["z"] - step)))
        elif index > last:
            there = dict(delta)
            there[axis] = 1
            hops.append((axis, 1, (there["x"], there["y"], there["z"])))
    return hops


def project_kernel(depth, n_seq, tok_ref, w_ref, meta_ref, out_ref, meta_out,
                   tok_all, w_all, meta_all, local_sem, pair_send, pair_recv,
                   meta_send, meta_recv, block_send, block_recv):
    z = lax.axis_index("dp")
    seq = lax.axis_index("seq")
    core = lax.rem(seq, CORES)
    plane = seq // CORES
    x = lax.rem(plane, 2)
    y = plane // 2
    rows, model = tok_ref.shape
    shard = w_ref.shape[0]
    half = out_ref.shape[1]
    heads_per = HEADS // CORES * HEAD_DIM
    kv_per = KV_HEADS // CORES * HEAD_DIM
    block_rows = shard * CORES
    partner = (z, seq + 1 - 2 * core)
    side = {
        "x": (z, (y * 2 + 1 - x) * CORES + core),
        "y": (z, ((1 - y) * 2 + x) * CORES + core),
    }

    def inside(dz):
        return (z + dz >= 0) & (z + dz < depth)

    barrier = pltpu.get_barrier_semaphore()
    for step in range(1, n_seq):
        pl.semaphore_signal(barrier, inc=1, device_id=(z, lax.rem(seq + step, n_seq)),
                            device_id_type=MESH)
    for step in (1, -1):
        @pl.when(inside(step))
        def _(step=step):
            pl.semaphore_signal(barrier, inc=1, device_id=(z + step, seq), device_id_type=MESH)
    peers = n_seq - 1 + jnp.where(z > 0, 1, 0) + jnp.where(z < depth - 1, 1, 0)
    pl.semaphore_wait(barrier, peers)

    def chip_of(offset):
        dx, dy, dz = offset
        cx = 1 - x if dx else x
        cy = 1 - y if dy else y
        return ((z + dz) * 2 + cy) * 2 + cx

    mine = chip_of((0, 0, 0))
    own_rows = pl.ds(pl.multiple_of(core * shard, shard), shard)
    slices = ((0, 0, heads_per), (HEADS * HEAD_DIM, heads_per, kv_per),
              ((HEADS + KV_HEADS) * HEAD_DIM, heads_per + kv_per, kv_per))
    first = []
    for index, (base, place, width) in enumerate(slices):
        there = pl.ds(pl.multiple_of(base + (1 - core) * width, 128), width)
        here = pl.ds(pl.multiple_of(base + core * width, 128), width)
        first.append(pltpu.make_async_remote_copy(
            src_ref=w_ref.at[:, there], dst_ref=w_all.at[mine, own_rows, pl.ds(place, width)],
            send_sem=pair_send.at[index], recv_sem=pair_recv.at[index],
            device_id=partner, device_id_type=MESH))
        first.append(pltpu.make_async_copy(
            w_ref.at[:, here], w_all.at[mine, own_rows, pl.ds(place, width)],
            local_sem.at[index]))
    for copy in first:
        copy.start()
    tok_rows = pl.ds(pl.multiple_of(core * rows, rows), rows)
    tok_send = pltpu.make_async_remote_copy(
        src_ref=tok_ref, dst_ref=tok_all.at[tok_rows, :], send_sem=pair_send.at[3],
        recv_sem=pair_recv.at[3], device_id=partner, device_id_type=MESH)
    tok_copy = pltpu.make_async_copy(tok_ref, tok_all.at[tok_rows, :], local_sem.at[3])
    for copy in first:
        copy.wait()

    ids = {}
    pending = []

    def block(part, offset):
        start, width = part_bounds(half)[part]
        return w_all.at[chip_of(offset), :, pl.ds(start, width)]

    def recv_index(part, offset):
        dx, dy, dz = offset
        return ((part * (2 * depth - 1) + dz + depth - 1) * 2 + dy) * 2 + dx

    def send(part, offset, hop):
        axis, step, there = hop
        key = (part, offset, axis, step)
        ids.setdefault(key, len(ids))
        target = side[axis] if axis != "z" else (z + step, seq)
        return pltpu.make_async_remote_copy(
            src_ref=block(part, offset), dst_ref=block(part, offset),
            send_sem=block_send.at[ids[key]], recv_sem=block_recv.at[recv_index(part, there)],
            device_id=target, device_id_type=MESH)

    def guarded(offset, hop, action):
        conds = []
        if offset[2]:
            conds.append(inside(offset[2]))
        if hop[0] == "z":
            conds.append(inside(hop[1]))
        if conds:
            pl.when(functools.reduce(lambda a, b: a & b, conds))(action)
        else:
            action()

    def start(part, offset, hop):
        guarded(offset, hop, lambda: send(part, offset, hop).start())
        pending.append((part, offset, hop))

    opening = [(part, hop) for part in range(3) for hop in forwards(ORDERS[part], (0, 0, 0), depth)]
    opening.sort(key=lambda item: ORDERS[item[0]].index(item[1][0]))
    for part, hop in opening:
        start(part, (0, 0, 0), hop)
    tok_send.start()
    tok_copy.start()
    others = []
    for step in range(1, n_seq):
        others.append(pltpu.make_async_remote_copy(
            src_ref=meta_ref, dst_ref=meta_all.at[seq], send_sem=meta_send.at[step],
            recv_sem=meta_recv.at[step], device_id=(z, lax.rem(seq + step, n_seq)),
            device_id_type=MESH))
        others[-1].start()

    def consume(part, offset, initial=False):
        begin, width = part_bounds(half)[part]
        chip = chip_of(offset)
        depth_cols = pl.ds(pl.multiple_of(chip * block_rows, block_rows), block_rows)
        tile = out_ref.shape[0] // 3

        @pl.loop(0, 3)
        def _(index):
            at = pl.ds(pl.multiple_of(index * tile, tile), tile)
            product = jnp.dot(tok_all[at, depth_cols], w_all[chip, :, pl.ds(begin, width)],
                              preferred_element_type=jnp.float32)
            if initial:
                out_ref[at, pl.ds(begin, width)] = product
            else:
                out_ref[at, pl.ds(begin, width)] += product

    def consume_guarded(part, offset):
        if offset[2]:
            pl.when(inside(offset[2]))(lambda: consume(part, offset))
        else:
            consume(part, offset)

    events = []
    for part in range(3):
        for dz in range(1 - depth, depth):
            for dy in range(2):
                for dx in range(2):
                    if (dx, dy, dz) != (0, 0, 0):
                        events.append((part, (dx, dy, dz)))

    def rank(event):
        part, offset = event
        hops = sum(abs(v) for v in offset)
        last = max(ORDERS[part].index(a) for a, v in zip("xyz", offset) if v)
        return (hops, last, part)

    events.sort(key=rank)
    lag = 6
    waiting = []
    ready = False

    def begin_products():
        tok_copy.wait()
        tok_send.wait()
        for part in range(3):
            consume(part, (0, 0, 0), initial=True)

    for part, offset in events:
        dz = offset[2]

        def arrive(part=part, offset=offset):
            own = block(part, offset)
            pltpu.make_async_remote_copy(
                src_ref=own, dst_ref=own, send_sem=block_send.at[0],
                recv_sem=block_recv.at[recv_index(part, offset)],
                device_id=partner, device_id_type=MESH).wait_recv()
        if dz:
            pl.when(inside(dz))(arrive)
        else:
            arrive()
        for hop in forwards(ORDERS[part], offset, depth):
            start(part, offset, hop)
        waiting.append((part, offset))
        if len(waiting) > lag:
            if not ready:
                begin_products()
                ready = True
            consume_guarded(*waiting.pop(0))
    if not ready:
        begin_products()
    for item in waiting:
        consume_guarded(*item)
    for copy in others:
        copy.wait()
    meta_all[seq] = meta_ref[...]
    meta_out[...] = meta_all[...]
    for part, offset, hop in pending:
        guarded(offset, hop, lambda: send(part, offset, hop).wait_send())


def count_sends(depth):
    total = 0
    for order in ORDERS:
        for dz in range(1 - depth, depth):
            for dy in range(2):
                for dx in range(2):
                    total += len(forwards(order, (dx, dy, dz), depth))
    return total


def project(token_rows, qkv_weight, meta):
    depth, n_seq = lax.axis_size("dp"), lax.axis_size("seq")
    rows, model = token_rows.shape
    columns = qkv_weight.shape[1]
    half = columns // CORES
    chips = depth * n_seq // CORES
    block_rows = model // chips
    sends = count_sends(depth)
    recvs = len(ORDERS) * (2 * depth - 1) * 4
    return pl.pallas_call(
        functools.partial(project_kernel, depth, n_seq),
        out_shape=(jax.ShapeDtypeStruct((CORES * rows, half), jnp.float32),
                   jax.ShapeDtypeStruct((n_seq,) + meta.shape, jnp.int32)),
        in_specs=[pl.BlockSpec(memory_space=pl.ANY), pl.BlockSpec(memory_space=pl.ANY),
                  pl.BlockSpec(memory_space=pltpu.VMEM)],
        out_specs=(pl.BlockSpec(memory_space=pltpu.VMEM), pl.BlockSpec(memory_space=pltpu.VMEM)),
        scratch_shapes=[
            pltpu.VMEM((CORES * rows, model), jnp.bfloat16),
            pltpu.VMEM((chips, block_rows, half), jnp.bfloat16),
            pltpu.VMEM((n_seq,) + meta.shape, jnp.int32),
            pltpu.SemaphoreType.DMA((4,)),
            pltpu.SemaphoreType.DMA((4,)),
            pltpu.SemaphoreType.DMA((4,)),
            pltpu.SemaphoreType.DMA((n_seq,)),
            pltpu.SemaphoreType.DMA((n_seq,)),
            pltpu.SemaphoreType.DMA((sends,)),
            pltpu.SemaphoreType.DMA((recvs,)),
        ],
        compiler_params=pltpu.CompilerParams(
            collective_id=0, has_side_effects=True, vmem_limit_bytes=44 * 2**20),
        cost_estimate=pl.CostEstimate(flops=2 * rows * model * columns,
                                      bytes_accessed=2 * model * columns, transcendentals=0),
    )(token_rows, qkv_weight, meta)


def project_plain(token_rows, qkv_weight, meta):
    n_seq = lax.axis_size("seq")
    core = lax.axis_index("seq") % CORES
    other = lax.ppermute(token_rows, "seq", [(i, i ^ 1) for i in range(n_seq)])
    pair = jnp.where(core == 0, jnp.concatenate([token_rows, other]),
                     jnp.concatenate([other, token_rows]))
    weight = lax.all_gather(qkv_weight, ("dp", "seq"), axis=0, tiled=True)
    heads_per = HEADS // CORES * HEAD_DIM
    kv_per = KV_HEADS // CORES * HEAD_DIM
    pieces = [
        lax.dynamic_slice_in_dim(weight, base + core * width, width, 1)
        for base, width in ((0, heads_per), (HEADS * HEAD_DIM, kv_per),
                            ((HEADS + KV_HEADS) * HEAD_DIM, kv_per))
    ]
    projected = jnp.dot(pair, jnp.concatenate(pieces, axis=1), preferred_element_type=jnp.float32)
    return projected, lax.all_gather(meta, "seq")


def positions(segment_ids, prefix_len):
    index_list = jnp.arange(segment_ids.shape[0], dtype=jnp.int32)
    fresh_doc = jnp.concatenate([jnp.ones((1,), jnp.bool_), segment_ids[1:] != segment_ids[:-1]])
    first_row = lax.cummax(jnp.where(fresh_doc, index_list, 0), axis=0)
    leading = segment_ids == segment_ids[0]
    return index_list - first_row + jnp.where(leading, prefix_len, 0)


def rotate(flat, position):
    rows, width = flat.shape
    heads = flat.reshape(rows, width // HEAD_DIM, HEAD_DIM)
    half_dim = HEAD_DIM // 2
    frequency = ROPE_BASE ** (-2.0 * jnp.arange(half_dim, dtype=jnp.float32) / HEAD_DIM)
    angles = position.astype(jnp.float32)[:, None] * frequency[None, :]
    cosine = jnp.cos(angles)[:, None, :]
    sine = jnp.sin(angles)[:, None, :]
    a, b = heads[..., :half_dim], heads[..., half_dim:]
    turned = jnp.concatenate([a * cosine - b * sine, b * cosine + a * sine], axis=-1)
    return turned.reshape(rows, width).astype(jnp.bfloat16)


def attend_kernel(tile, reach_ref, prefix_ref, q_ref, k_ref, v_ref, col_ref, row_ref, out_ref):
    block = pl.program_id(0)
    count = q_ref.shape[1]
    group = q_ref.shape[2] // HEAD_DIM
    prefix = prefix_ref[block]
    factor = HEAD_DIM ** -0.5 * 1.4426950408889634

    def run(index, remote):
        at = pl.ds(pl.multiple_of(index * tile, tile), tile)
        blocks = remote + 1
        window = pl.ds(block + REACH - remote, blocks)
        keys = k_ref[window].reshape(blocks * count, HEAD_DIM)
        values = v_ref[window].reshape(blocks * count, HEAD_DIM)
        ids = col_ref[0, at, :]
        columns = lax.broadcasted_iota(jnp.int32, (tile, count), 1)
        lines = lax.broadcasted_iota(jnp.int32, (tile, count), 0) + index * tile
        seen = (columns <= lines) & (row_ref[0] == ids)
        if remote:
            back = lax.broadcasted_iota(jnp.int32, (tile, remote * count), 1) - remote * count
            lead = ids == row_ref[0][:, :1]
            seen = jnp.concatenate([(back >= -prefix) & lead, seen], axis=1)
        for head in range(group):
            cols = pl.ds(head * HEAD_DIM, HEAD_DIM)
            scores = lax.dot_general(q_ref[0, at, cols], keys, (((1,), (1,)), ((), ())),
                                     preferred_element_type=jnp.float32)
            scores = jnp.where(seen, scores, MASKED)
            top = jnp.max(scores, axis=-1, keepdims=True)
            expo = jnp.exp2((scores - top) * factor)
            total = jnp.sum(expo, axis=-1, keepdims=True)
            probs = (expo * (1.0 / total)).astype(jnp.bfloat16)
            out_ref[0, at, cols] = jnp.dot(
                probs, values, preferred_element_type=jnp.float32).astype(jnp.bfloat16)

    @pl.loop(0, count // tile)
    def _(index):
        remote = reach_ref[block, index]
        for blocks in range(REACH + 1):
            low = remote > (blocks - 1) * count
            high = remote <= blocks * count
            cond = low & high if 0 < blocks < REACH else (high if blocks == 0 else low)
            pl.when(cond)(functools.partial(run, index, blocks))


def attend(queries, keys, values, segs, prefix):
    blocks, count, width = queries.shape
    kv_heads = keys.shape[2] // HEAD_DIM
    group = width // kv_heads
    tile = 128
    starts = segs[:, ::tile]
    reach = jnp.where(starts == segs[:, :1], prefix[:, None], 0)
    smem = pl.BlockSpec(memory_space=pltpu.SMEM)
    return pl.pallas_call(
        functools.partial(attend_kernel, tile),
        grid=(blocks, kv_heads),
        out_shape=jax.ShapeDtypeStruct(queries.shape, jnp.bfloat16),
        in_specs=[
            smem, smem,
            pl.BlockSpec((1, count, group), lambda b, h: (b, 0, h)),
            pl.BlockSpec((keys.shape[0], count, HEAD_DIM), lambda b, h: (0, 0, h)),
            pl.BlockSpec((keys.shape[0], count, HEAD_DIM), lambda b, h: (0, 0, h)),
            pl.BlockSpec((1, count, 1), lambda b, h: (b, 0, 0)),
            pl.BlockSpec((1, 1, count), lambda b, h: (b, 0, 0)),
        ],
        out_specs=pl.BlockSpec((1, count, group), lambda b, h: (b, 0, h)),
        compiler_params=pltpu.CompilerParams(vmem_limit_bytes=32 * 2**20),
        cost_estimate=pl.CostEstimate(
            flops=4 * blocks * count * width * count * (REACH + 1),
            bytes_accessed=8 * blocks * count * width, transcendentals=0),
    )(reach, prefix, queries, keys, values, segs[:, :, None], segs[:, None, :])


def on_device(tokens, qkv_weight, segments, destination, doc_prefix):
    n_seq = lax.axis_size("seq")
    me = lax.axis_index("seq")
    count = tokens.shape[1]
    meta = jnp.zeros((META_ROWS, count), jnp.int32)
    meta = meta.at[0].set(segments[0]).at[1].set(destination[0]).at[2].set(doc_prefix[0, 0])
    planar = n_seq == 4 * CORES
    projected, metas = (project if planar else project_plain)(tokens[0], qkv_weight, meta)

    pair = lax.dynamic_slice_in_dim(metas, me // CORES * CORES, CORES, 0)
    segs, prefix = pair[:, 0], pair[:, 2, 0]
    targets = pair[:, 1]
    heads_per = HEADS // CORES * HEAD_DIM
    kv_per = KV_HEADS // CORES * HEAD_DIM
    position = jax.vmap(positions)(segs, prefix).reshape(-1)
    keys = rotate(projected[:, heads_per : heads_per + kv_per], position)
    values = projected[:, heads_per + kv_per :].astype(jnp.bfloat16)
    own = jnp.concatenate([keys, values], axis=1)
    before = lax.ppermute(own, "seq", [(i, i + CORES) for i in range(n_seq - CORES)])
    queries = rotate(projected[:, :heads_per], position).reshape(CORES, count, heads_per)
    span = jnp.concatenate([before, own]).reshape(2 * CORES, count, 2 * kv_per)
    heads_out = attend(queries, span[:, :, :kv_per], span[:, :, kv_per:], segs, prefix)

    capacity = count // min(n_seq, 16)
    slots = jnp.arange(n_seq * capacity, dtype=jnp.int32)

    def pick(target, rows):
        owner = target // count
        one_hot = (owner[:, None] == jnp.arange(n_seq, dtype=jnp.int32)[None, :]).astype(jnp.int32)
        order = jnp.sum(jnp.cumsum(one_hot, axis=0) * one_hot, axis=1) - 1
        chosen = (slots[:, None] == (owner * capacity + order)[None, :]).astype(jnp.bfloat16)
        return jnp.dot(chosen, rows, preferred_element_type=jnp.float32).astype(jnp.bfloat16)

    send_rows = jnp.stack(
        [pick(targets[j], heads_out[j]).reshape(n_seq, capacity, heads_per) for j in range(CORES)],
        axis=1)
    got = lax.all_to_all(send_rows, "seq", split_axis=0, concat_axis=0, tiled=True)
    got = got.reshape(n_seq // CORES, CORES, CORES, capacity, heads_per)

    everyone = metas[:, 1]
    ours = everyone // count == me
    order = jnp.cumsum(ours.astype(jnp.int32), axis=1) - 1
    match = ours[:, None, :] & (
        order[:, None, :] == jnp.arange(capacity, dtype=jnp.int32)[None, :, None])
    places = jnp.sum(jnp.where(match, everyone[:, None, :] % count + 1, 0), axis=2) - 1
    put = (jnp.arange(count, dtype=jnp.int32)[:, None] == places.reshape(1, -1)).astype(jnp.bfloat16)
    halves = [
        jnp.dot(put, got[:, c].reshape(n_seq * capacity, heads_per),
                preferred_element_type=jnp.float32).astype(jnp.bfloat16)
        for c in range(CORES)
    ]
    return jnp.concatenate(halves, axis=1)[None]


def solution(mesh):
    placed = (
        P("dp", "seq", None),
        P(("dp", "seq"), None),
        P("dp", "seq"),
        P("dp", "seq"),
        P("dp", "seq"),
    )
    return jax.shard_map(
        on_device, mesh=mesh, in_specs=placed, out_specs=P("dp", "seq", None), check_vma=False
    )
```

time: 299 us -> 201 us (0.67)
  waiting for transfers between devices: 172 us -> 19.3 us
  Pallas kernels: 0 us -> 134 us
  matrix products: 46.7 us -> 2.31 us
  between operations: 14.5 us -> 0.96 us
  starting transfers between devices: 20.1 us -> 8.11 us
  local copies, waits for them, and re-layouts: 27.1 us -> 18 us
    all_gather x1 -> x0, waiting for transfers between devices: 152 us -> none  [on_device(): lax.all_gather(qkv_weight, ('dp', 'seq'), axis=0, tiled=True)]
    pallas_call x0 -> x2, Pallas kernels: none -> 134 us  [the longest x1 113 us: project(): pl.pallas_call(functools.partial(project_kernel, depth, n_seq), out_shape...]
    dot_general x5 -> x4, matrix products: 32 us -> 2.31 us  [the longest x2 1.15 us: pick(): jnp.dot(chosen, rows, preferred_element_type=jnp.float32)]
    sub x4 -> x0, matrix products: 14.7 us -> none  [head_block(): expo = jnp.exp(scores - top_score)]
    scatter x3, local copies, waits for them, and re-layouts: 12 us -> 1.44 us  [on_device(): meta.at[0].set(segments[0]).at[1].set(destination[0]).at[2]]
    all_to_all x1, starting transfers between devices: 9.86 us -> 3.89 us  [on_device(): lax.all_to_all(send_rows, 'seq', split_axis=0, concat_axis=0, tiled=True)]
    or x4 -> x0, other arithmetic: 5.15 us -> none  [visible_keys(): return local_part | remote_part]
    another operation x6 -> x12, other arithmetic: 3.13 us -> 7.63 us
  transfers between devices with their start and end apart: 5 -> 2, of which waited for: 2 -> 1; matrix products, arithmetic and copies ran while one was open for 22% -> 9% of each run, Pallas kernels for 0% -> 0%
where the time goes in v1:
time: 201 us; the launch traced here: 200 us
  Pallas kernels  134 us (67%)
  waiting for transfers between devices  19.3 us (10%)
  local copies, waits for them, and re-layouts  18 us (9%)
  other arithmetic  16.6 us (8%)
  starting transfers between devices  8.11 us (4%)
  matrix products  2.31 us (1%)
    pallas_call x1, Pallas kernels, project(): pl.pallas_call(functools.partial(project_kernel, depth, n_seq), out_shape...  113 us
    pallas_call x1, Pallas kernels, attend(): pl.pallas_call(functools.partial(attend_kernel, tile), grid=(blocks, kv_h...  21.7 us
    all_to_all x1, waiting for transfers between devices, on_device(): lax.all_to_all(send_rows, 'seq', split_axis=0, concat_axis=0, tiled=True)  19.3 us
    unnamed x12, local copies, waits for them, and re-layouts  11.5 us
    another operation x10, other arithmetic  6.27 us
    ppermute x1, starting transfers between devices, on_device(): lax.ppermute(own, 'seq', [(i, i + CORES) for i in range(n_seq - CORES)])  4.23 us
  transfers between devices with their start and end apart: 2, of which 1 were waited for; matrix products, arithmetic and copies ran while one was open for 9% of the time, Pallas kernels for 0%

profile of v1, /device:TPU:0, one launch (start us, length us, event | category | flops | bytes accessed | tf_op | source)
XLA Modules:
  0.0 199.6 jit_solution(6350292368866397296)
XLA Ops:
  0.7 0.7 scatter.10
  1.4 0.7 scatter.11
  2.1 0.0 copy-start.1
  2.1 1.9 copy-done.1
  4.0 0.0 copy-start.2
  4.0 1.1 copy-done.2
  5.2 112.6 %shard_map.55 = (f32[768,1536]{1,0:T(8,128)S(1)}, s32[8,8,384]{2,1,0:T(8,128)S(1)}) custom-call(bf16[384,4096]{1,0:T(8,128)(2,1)S(1)} %bitcast.73, bf16[128,3072]{1,0:T(8,128)(2,1)S(1)} %copy-done.2, s32[8,384]{1,0:T(8,128)S(1)} %scatter.14.meta_ref), custom_call_target="tpu_custom_call" | custom-call | flops 9663676416 | bytes 25165824 | tf_op jit(solution)/shard_map/pallas_call | solution.py:262
  117.8 0.0 copy-start
  117.8 0.1 slice_reduce_fusion.4
  117.9 0.1 slice_compare_fusion
  118.0 0.1 slice.213
  118.1 1.8 copy-done
  119.9 0.1 slice.158
  120.0 0.1 dynamic-slice_reduce_fusion.prefix_ref
  120.1 0.1 broadcast_in_dim.83
  120.2 0.1 pad_select_fusion
  120.3 0.6 reduce-window.34
  120.9 0.2 slice_reduce_fusion.3
  121.1 0.2 reduce-window.35
  121.3 0.1 broadcast_maximum_fusion
  121.4 0.1 eq.155
  121.5 0.4 reshape.400
  121.9 1.4 multiply_cosine_fusion
  123.4 1.4 subtract_convert_fusion.1
  124.8 1.1 pad_maximum_fusion.3
  125.8 0.1 copy.36
  125.9 1.0 pad_maximum_fusion.2
  126.9 4.2 %collective-permute-start = (bf16[768,512]{1,0:T(8,128)(2,1)}, bf16[768,512]{1,0:T(8,128)(2,1)}, u32[]{:S(2)}, u32[]{:S(2)}) collective-permute-start(bf16[768,512]{1,0:T(8,128)(2,1)} %pad_maximum_fusion.2), channel_id=1, source_target_pairs={{0,2},{1,3},{2,4},{3,5},{4,6},{5,7},{8,10},{9,11},{10,12},{11,13},... | collective-permute-start | bytes 2359304 | tf_op jit(solution)/shard_map/ppermute | solution.py:416
  131.2 0.1 slice.148
  131.3 4.0 %slice_bitcast_fusion = f32[96,8,8,128]{3,1,2,0:T(8,128)} fusion(f32[768,1536]{1,0:T(8,128)} %copy-done), kind=kLoop, calls=%fused_computation.2 | loop fusion | bytes 6291456
  135.3 0.8 reduce-window.36
  136.2 0.2 slice_reduce_fusion
  136.4 0.9 reduce-window.30
  137.3 0.2 slice_reduce_fusion.1
  137.5 0.2 copy.20.col_ref
  137.7 2.6 %copy.26 = f32[96,8,8,128]{3,2,1,0:T(8,128)S(1)} copy(f32[96,8,8,128]{3,1,2,0:T(8,128)} %slice_bitcast_fusion) | data formatting | bytes 6291456
  140.4 1.4 subtract_convert_fusion
  141.8 2.0 %pad_maximum_fusion = bf16[768,8,128]{2,1,0:T(8,128)(2,1)} fusion(bf16[768,8,64]{2,1,0:T(8,128)(2,1)S(1)} %get-tuple-element.55, bf16[768,8,64]{2,1,0:T(8,128)(2,1)S(1)} %get-tuple-element.54), kind=kLoop, calls=%fused_computation.3 | loop fusion | flops 3145728 | bytes 3145728 | tf_op jit(solution)/shard_map/concatenate | solution.py:323
  143.8 2.5 %convert_element_type.50.q_ref = bf16[2,384,1024]{2,1,0:T(8,128)(2,1)S(1)} reshape(bf16[768,8,128]{2,1,0:T(8,128)(2,1)} %pad_maximum_fusion) | data formatting | bytes 3145728 | tf_op jit(solution)/shard_map/convert_element_type | solution.py:324
  146.3 0.1 fusion.8
  146.4 0.1 fusion.9
  146.5 0.1 compare_select_fusion.reach_ref
  146.6 0.0 collective-permute-done
  146.6 1.2 maximum_maximum_fusion
  147.8 0.1 fusion.15
  148.0 21.7 %shard_map.56 = bf16[2,384,1024]{2,1,0:T(8,128)(2,1)S(1)} custom-call(s32[2,3]{1,0:T(2,128)S(1)} %compare_select_fusion.reach_ref, s32[2]{0:T(128)S(1)} %dynamic-slice_reduce_fusion.prefix_ref, bf16[2,384,1024]{2,1,0:T(8,128)(2,1)S(1)} %convert_element_type.50.q_ref, bf16[4,384,256]{2,1,0:T(8,128)(2,1)S(1)} %get-tuple-element.59.k_ref, ...), custom_call_target="tpu_custom_call" | custom-call | flops 3623878656 | bytes 6291456 | tf_op jit(solution)/shard_map/pallas_call | solution.py:378
  169.6 0.6 convolution_convert_fusion.2
  170.2 0.6 convolution_convert_fusion.3
  170.8 1.3 pad_maximum_fusion.1
  172.1 3.9 %all-to-all-start = ((bf16[8,2,48,1024]{3,2,1,0:T(8,128)(2,1)}), bf16[8,2,48,1024]{3,2,1,0:T(8,128)(2,1)S(1)}, u32[]{:S(2)}, u32[]{:S(2)}) async-start(bf16[8,2,48,1024]{3,2,1,0:T(8,128)(2,1)} %pad_maximum_fusion.1), calls=%async_computation | async-start | bytes 3145728 | tf_op jit(solution)/shard_map/all_to_all | solution.py:434
  176.0 0.1 fusion.5
  176.1 0.1 fusion.7
  176.2 0.9 reduce-window.26
  177.1 0.2 slice_reduce_fusion.2
  177.3 0.1 add_bitcast_fusion
  177.4 0.2 select_reduce_fusion
  177.7 0.1 sub.70
  177.7 19.3 %all-to-all-done = bf16[8,2,48,1024]{3,2,1,0:T(8,128)(2,1)S(1)} async-done(((bf16[8,2,48,1024]{3,2,1,0:T(8,128)(2,1)}), bf16[8,2,48,1024]{3,2,1,0:T(8,128)(2,1)S(1)}, u32[]{:S(2)}, u32[]{:S(2)}) %all-to-all-start) | async-done | bytes 1572896 | tf_op jit(solution)/shard_map/all_to_all | solution.py:434
  197.0 0.2 fusion.14
  197.2 0.6 convolution_convert_fusion.1
  197.8 0.6 convolution_convert_fusion
  198.4 1.2 maximum_bitcast_fusion
  (28 shorter events, 0.4 us)
Async XLA Ops:
  2.1 1.9 copy-start.1
  4.0 1.1 copy-start.2
  117.8 2.1 %copy-start = (f32[768,1536]{1,0:T(8,128)}, f32[768,1536]{1,0:T(8,128)S(1)}, u32[]{:S(2)}) copy-start(f32[768,1536]{1,0:T(8,128)S(1)} %get-tuple-element.44) | copy-start | bytes 14155780
  126.9 19.7 %collective-permute-start = (bf16[768,512]{1,0:T(8,128)(2,1)}, bf16[768,512]{1,0:T(8,128)(2,1)}, u32[]{:S(2)}, u32[]{:S(2)}) collective-permute-start(bf16[768,512]{1,0:T(8,128)(2,1)} %pad_maximum_fusion.2), channel_id=1, source_target_pairs={{0,2},{1,3},{2,4},{3,5},{4,6},{5,7},{8,10},{9,11},{10,12},{11,13},... | collective-permute-start | bytes 2359304 | tf_op jit(solution)/shard_map/ppermute | solution.py:416
  172.1 24.9 %all-to-all-start = ((bf16[8,2,48,1024]{3,2,1,0:T(8,128)(2,1)}), bf16[8,2,48,1024]{3,2,1,0:T(8,128)(2,1)S(1)}, u32[]{:S(2)}, u32[]{:S(2)}) async-start(bf16[8,2,48,1024]{3,2,1,0:T(8,128)(2,1)} %pad_maximum_fusion.1), calls=%async_computation | async-start | bytes 3145728 | tf_op jit(solution)/shard_map/all_to_all | solution.py:434

commit v2 on v1

--- a/solution.py
+++ b/solution.py
@@ -17,12 +17,13 @@
 MESH = pl.DeviceIdType.MESH
 META_ROWS = 8
 
-ORDERS = ("zyx", "zxy", "xyz")
+ORDERS = ("zxy", "zyx", "xyz")
+HEAD_START = (2.5, 0, 0)
 
 
 def part_bounds(width):
     unit = width // 12
-    return ((0, 5 * unit), (5 * unit, 4 * unit), (9 * unit, 3 * unit))
+    return ((0, 4 * unit), (4 * unit, 5 * unit), (9 * unit, 3 * unit))
 
 
 def forwards(order, offset, depth):
@@ -44,9 +45,9 @@
     return hops
 
 
-def project_kernel(depth, n_seq, tok_ref, w_ref, meta_ref, out_ref, meta_out,
-                   tok_all, w_all, meta_all, local_sem, pair_send, pair_recv,
-                   meta_send, meta_recv, block_send, block_recv):
+def project_kernel(depth, n_seq, tok_ref, w_ref, meta_ref, turn_ref, query_out, kv_out, meta_out,
+                   tok_all, w_all, meta_all, turn_all, total, kv_before, local_sem, pair_send,
+                   pair_recv, meta_send, meta_recv, block_send, block_recv, kv_send, kv_recv):
     z = lax.axis_index("dp")
     seq = lax.axis_index("seq")
     core = lax.rem(seq, CORES)
@@ -55,7 +56,8 @@
     y = plane // 2
     rows, model = tok_ref.shape
     shard = w_ref.shape[0]
-    half = out_ref.shape[1]
+    half = total.shape[1]
+    planes = n_seq // CORES
     heads_per = HEADS // CORES * HEAD_DIM
     kv_per = KV_HEADS // CORES * HEAD_DIM
     block_rows = shard * CORES
@@ -64,6 +66,7 @@
         "x": (z, (y * 2 + 1 - x) * CORES + core),
         "y": (z, ((1 - y) * 2 + x) * CORES + core),
     }
+    follower = (z, lax.rem(seq + CORES, n_seq))
 
     def inside(dz):
         return (z + dz >= 0) & (z + dz < depth)
@@ -87,8 +90,9 @@
 
     mine = chip_of((0, 0, 0))
     own_rows = pl.ds(pl.multiple_of(core * shard, shard), shard)
-    slices = ((0, 0, heads_per), (HEADS * HEAD_DIM, heads_per, kv_per),
-              ((HEADS + KV_HEADS) * HEAD_DIM, heads_per + kv_per, kv_per))
+    slices = ((HEADS * HEAD_DIM, 0, kv_per),
+              ((HEADS + KV_HEADS) * HEAD_DIM, kv_per, kv_per),
+              (0, 2 * kv_per, heads_per))
     first = []
     for index, (base, place, width) in enumerate(slices):
         there = pl.ds(pl.multiple_of(base + (1 - core) * width, 128), width)
@@ -107,6 +111,10 @@
         src_ref=tok_ref, dst_ref=tok_all.at[tok_rows, :], send_sem=pair_send.at[3],
         recv_sem=pair_recv.at[3], device_id=partner, device_id_type=MESH)
     tok_copy = pltpu.make_async_copy(tok_ref, tok_all.at[tok_rows, :], local_sem.at[3])
+    turn_send = pltpu.make_async_remote_copy(
+        src_ref=turn_ref, dst_ref=turn_all.at[tok_rows, :], send_sem=pair_send.at[4],
+        recv_sem=pair_recv.at[4], device_id=partner, device_id_type=MESH)
+    turn_copy = pltpu.make_async_copy(turn_ref, turn_all.at[tok_rows, :], local_sem.at[4])
     for copy in first:
         copy.wait()
 
@@ -152,6 +160,8 @@
         start(part, (0, 0, 0), hop)
     tok_send.start()
     tok_copy.start()
+    turn_send.start()
+    turn_copy.start()
     others = []
     for step in range(1, n_seq):
         others.append(pltpu.make_async_remote_copy(
@@ -164,7 +174,7 @@
         begin, width = part_bounds(half)[part]
         chip = chip_of(offset)
         depth_cols = pl.ds(pl.multiple_of(chip * block_rows, block_rows), block_rows)
-        tile = out_ref.shape[0] // 3
+        tile = total.shape[0] // 3
 
         @pl.loop(0, 3)
         def _(index):
@@ -172,9 +182,9 @@
             product = jnp.dot(tok_all[at, depth_cols], w_all[chip, :, pl.ds(begin, width)],
                               preferred_element_type=jnp.float32)
             if initial:
-                out_ref[at, pl.ds(begin, width)] = product
+                total[at, pl.ds(begin, width)] = product
             else:
-                out_ref[at, pl.ds(begin, width)] += product
+                total[at, pl.ds(begin, width)] += product
 
     def consume_guarded(part, offset):
         if offset[2]:
@@ -194,7 +204,7 @@
         part, offset = event
         hops = sum(abs(v) for v in offset)
         last = max(ORDERS[part].index(a) for a, v in zip("xyz", offset) if v)
-        return (hops, last, part)
+        return (hops - HEAD_START[part], last, part)
 
     events.sort(key=rank)
     lag = 6
@@ -204,9 +214,37 @@
     def begin_products():
         tok_copy.wait()
         tok_send.wait()
+        turn_copy.wait()
+        turn_send.wait()
         for part in range(3):
             consume(part, (0, 0, 0), initial=True)
 
+    def turned(at, begin):
+        heads = total[at, pl.ds(begin, HEAD_DIM)]
+        swapped = pltpu.roll(heads, HEAD_DIM // 2, 1)
+        angle = turn_all[at, :]
+        return (heads * angle[:, :HEAD_DIM] + swapped * angle[:, HEAD_DIM:]).astype(jnp.bfloat16)
+
+    kv_copy = pltpu.make_async_remote_copy(
+        src_ref=kv_out.at[pl.ds(CORES, CORES)], dst_ref=kv_before, send_sem=kv_send,
+        recv_sem=kv_recv, device_id=follower, device_id_type=MESH)
+
+    def share_kv():
+        for index in range(CORES):
+            at = pl.ds(index * rows, rows)
+            for begin in range(0, kv_per, HEAD_DIM):
+                kv_out[CORES + index, :, pl.ds(begin, HEAD_DIM)] = turned(at, begin)
+            kv_out[CORES + index, :, pl.ds(kv_per, kv_per)] = total[
+                at, pl.ds(kv_per, kv_per)].astype(jnp.bfloat16)
+        pl.when(plane < planes - 1)(lambda: kv_copy.start())
+
+    def use(item):
+        consume_guarded(*item)
+        left[item[0]] -= 1
+        if item[0] == 0 and left[0] == 0:
+            share_kv()
+
+    left = [sum(1 for event in events if event[0] == part) for part in range(3)]
     for part, offset in events:
         dz = offset[2]
 
@@ -227,15 +265,30 @@
             if not ready:
                 begin_products()
                 ready = True
-            consume_guarded(*waiting.pop(0))
+            use(waiting.pop(0))
     if not ready:
         begin_products()
     for item in waiting:
-        consume_guarded(*item)
+        use(item)
+    for index in range(CORES):
+        at = pl.ds(index * rows, rows)
+        for begin in range(0, heads_per, HEAD_DIM):
+            query_out[index, :, pl.ds(begin, HEAD_DIM)] = turned(at, 2 * kv_per + begin)
     for copy in others:
         copy.wait()
     meta_all[seq] = meta_ref[...]
     meta_out[...] = meta_all[...]
+
+    @pl.when(plane > 0)
+    def _():
+        kv_copy.wait_recv()
+        kv_out[0:CORES] = kv_before[...]
+
+    @pl.when(plane == 0)
+    def _():
+        kv_out[0:CORES] = jnp.zeros_like(kv_before)
+
+    pl.when(plane < planes - 1)(lambda: kv_copy.wait_send())
     for part, offset, hop in pending:
         guarded(offset, hop, lambda: send(part, offset, hop).wait_send())
 
@@ -250,47 +303,60 @@
     return total
 
 
-def project(token_rows, qkv_weight, meta):
+def project(token_rows, qkv_weight, meta, turn):
     depth, n_seq = lax.axis_size("dp"), lax.axis_size("seq")
     rows, model = token_rows.shape
     columns = qkv_weight.shape[1]
     half = columns // CORES
+    queries = HEADS // CORES * HEAD_DIM
+    kv_width = half - queries
     chips = depth * n_seq // CORES
     block_rows = model // chips
     sends = count_sends(depth)
     recvs = len(ORDERS) * (2 * depth - 1) * 4
+    vmem = pl.BlockSpec(memory_space=pltpu.VMEM)
     return pl.pallas_call(
         functools.partial(project_kernel, depth, n_seq),
-        out_shape=(jax.ShapeDtypeStruct((CORES * rows, half), jnp.float32),
+        out_shape=(jax.ShapeDtypeStruct((CORES, rows, queries), jnp.bfloat16),
+                   jax.ShapeDtypeStruct((2 * CORES, rows, kv_width), jnp.bfloat16),
                    jax.ShapeDtypeStruct((n_seq,) + meta.shape, jnp.int32)),
         in_specs=[pl.BlockSpec(memory_space=pl.ANY), pl.BlockSpec(memory_space=pl.ANY),
-                  pl.BlockSpec(memory_space=pltpu.VMEM)],
-        out_specs=(pl.BlockSpec(memory_space=pltpu.VMEM), pl.BlockSpec(memory_space=pltpu.VMEM)),
+                  vmem, vmem],
+        out_specs=(vmem, vmem, vmem),
         scratch_shapes=[
             pltpu.VMEM((CORES * rows, model), jnp.bfloat16),
             pltpu.VMEM((chips, block_rows, half), jnp.bfloat16),
             pltpu.VMEM((n_seq,) + meta.shape, jnp.int32),
-            pltpu.SemaphoreType.DMA((4,)),
-            pltpu.SemaphoreType.DMA((4,)),
-            pltpu.SemaphoreType.DMA((4,)),
+            pltpu.VMEM((CORES * rows, 2 * HEAD_DIM), jnp.float32),
+            pltpu.VMEM((CORES * rows, half), jnp.float32),
+            pltpu.VMEM((CORES, rows, kv_width), jnp.bfloat16),
+            pltpu.SemaphoreType.DMA((5,)),
+            pltpu.SemaphoreType.DMA((5,)),
+            pltpu.SemaphoreType.DMA((5,)),
             pltpu.SemaphoreType.DMA((n_seq,)),
             pltpu.SemaphoreType.DMA((n_seq,)),
             pltpu.SemaphoreType.DMA((sends,)),
             pltpu.SemaphoreType.DMA((recvs,)),
+            pltpu.SemaphoreType.DMA,
+            pltpu.SemaphoreType.DMA,
         ],
         compiler_params=pltpu.CompilerParams(
-            collective_id=0, has_side_effects=True, vmem_limit_bytes=44 * 2**20),
+            collective_id=0, has_side_effects=True, vmem_limit_bytes=60 * 2**20),
         cost_estimate=pl.CostEstimate(flops=2 * rows * model * columns,
                                       bytes_accessed=2 * model * columns, transcendentals=0),
-    )(token_rows, qkv_weight, meta)
-
-
-def project_plain(token_rows, qkv_weight, meta):
+    )(token_rows, qkv_weight, meta, turn)
+
+
+def project_plain(token_rows, qkv_weight, meta, turn):
     n_seq = lax.axis_size("seq")
+    rows = token_rows.shape[0]
     core = lax.axis_index("seq") % CORES
-    other = lax.ppermute(token_rows, "seq", [(i, i ^ 1) for i in range(n_seq)])
-    pair = jnp.where(core == 0, jnp.concatenate([token_rows, other]),
-                     jnp.concatenate([other, token_rows]))
+
+    def paired(block):
+        other = lax.ppermute(block, "seq", [(i, i ^ 1) for i in range(n_seq)])
+        return jnp.where(core == 0, jnp.concatenate([block, other]),
+                         jnp.concatenate([other, block]))
+
     weight = lax.all_gather(qkv_weight, ("dp", "seq"), axis=0, tiled=True)
     heads_per = HEADS // CORES * HEAD_DIM
     kv_per = KV_HEADS // CORES * HEAD_DIM
@@ -299,29 +365,36 @@
         for base, width in ((0, heads_per), (HEADS * HEAD_DIM, kv_per),
                             ((HEADS + KV_HEADS) * HEAD_DIM, kv_per))
     ]
-    projected = jnp.dot(pair, jnp.concatenate(pieces, axis=1), preferred_element_type=jnp.float32)
-    return projected, lax.all_gather(meta, "seq")
-
-
-def positions(segment_ids, prefix_len):
+    projected = jnp.dot(paired(token_rows), jnp.concatenate(pieces, axis=1),
+                        preferred_element_type=jnp.float32)
+    angle = paired(turn)
+
+    def turned(flat):
+        heads = flat.reshape(flat.shape[0], -1, HEAD_DIM)
+        swapped = jnp.roll(heads, HEAD_DIM // 2, axis=2)
+        both = heads * angle[:, None, :HEAD_DIM] + swapped * angle[:, None, HEAD_DIM:]
+        return both.reshape(flat.shape).astype(jnp.bfloat16)
+
+    queries = turned(projected[:, :heads_per]).reshape(CORES, rows, heads_per)
+    keys = turned(projected[:, heads_per : heads_per + kv_per])
+    values = projected[:, heads_per + kv_per :].astype(jnp.bfloat16)
+    own = jnp.concatenate([keys, values], axis=1)
+    before = lax.ppermute(own, "seq", [(i, i + CORES) for i in range(n_seq - CORES)])
+    span = jnp.concatenate([before, own]).reshape(2 * CORES, rows, 2 * kv_per)
+    return queries, span, lax.all_gather(meta, "seq")
+
+
+def turns(segment_ids, prefix_len):
+    first_row = jnp.sum(
+        (segment_ids[None, :] < segment_ids[:, None]).astype(jnp.int32), axis=1)
     index_list = jnp.arange(segment_ids.shape[0], dtype=jnp.int32)
-    fresh_doc = jnp.concatenate([jnp.ones((1,), jnp.bool_), segment_ids[1:] != segment_ids[:-1]])
-    first_row = lax.cummax(jnp.where(fresh_doc, index_list, 0), axis=0)
     leading = segment_ids == segment_ids[0]
-    return index_list - first_row + jnp.where(leading, prefix_len, 0)
-
-
-def rotate(flat, position):
-    rows, width = flat.shape
-    heads = flat.reshape(rows, width // HEAD_DIM, HEAD_DIM)
+    position = index_list - first_row + jnp.where(leading, prefix_len, 0)
     half_dim = HEAD_DIM // 2
     frequency = ROPE_BASE ** (-2.0 * jnp.arange(half_dim, dtype=jnp.float32) / HEAD_DIM)
     angles = position.astype(jnp.float32)[:, None] * frequency[None, :]
-    cosine = jnp.cos(angles)[:, None, :]
-    sine = jnp.sin(angles)[:, None, :]
-    a, b = heads[..., :half_dim], heads[..., half_dim:]
-    turned = jnp.concatenate([a * cosine - b * sine, b * cosine + a * sine], axis=-1)
-    return turned.reshape(rows, width).astype(jnp.bfloat16)
+    cosine, sine = jnp.cos(angles), jnp.sin(angles)
+    return jnp.concatenate([cosine, cosine, -sine, sine], axis=1)
 
 
 def attend_kernel(tile, reach_ref, prefix_ref, q_ref, k_ref, v_ref, col_ref, row_ref, out_ref):
@@ -345,17 +418,20 @@
             back = lax.broadcasted_iota(jnp.int32, (tile, remote * count), 1) - remote * count
             lead = ids == row_ref[0][:, :1]
             seen = jnp.concatenate([(back >= -prefix) & lead, seen], axis=1)
-        for head in range(group):
-            cols = pl.ds(head * HEAD_DIM, HEAD_DIM)
-            scores = lax.dot_general(q_ref[0, at, cols], keys, (((1,), (1,)), ((), ())),
-                                     preferred_element_type=jnp.float32)
-            scores = jnp.where(seen, scores, MASKED)
-            top = jnp.max(scores, axis=-1, keepdims=True)
-            expo = jnp.exp2((scores - top) * factor)
-            total = jnp.sum(expo, axis=-1, keepdims=True)
-            probs = (expo * (1.0 / total)).astype(jnp.bfloat16)
-            out_ref[0, at, cols] = jnp.dot(
-                probs, values, preferred_element_type=jnp.float32).astype(jnp.bfloat16)
+        parts = [pl.ds(head * HEAD_DIM, HEAD_DIM) for head in range(group)]
+        queries = jnp.concatenate([q_ref[0, at, cols] for cols in parts], axis=0)
+        scores = lax.dot_general(queries, keys, (((1,), (1,)), ((), ())),
+                                 preferred_element_type=jnp.float32)
+        scores = scores.reshape(group, tile, blocks * count)
+        scores = jnp.where(seen[None], scores, MASKED)
+        top = jnp.max(scores, axis=-1, keepdims=True)
+        expo = jnp.exp2((scores - top) * factor)
+        total = jnp.sum(expo, axis=-1, keepdims=True)
+        probs = (expo * (1.0 / total)).astype(jnp.bfloat16)
+        out = jnp.dot(probs.reshape(group * tile, blocks * count), values,
+                      preferred_element_type=jnp.float32).astype(jnp.bfloat16)
+        for head, cols in enumerate(parts):
+            out_ref[0, at, cols] = out[head * tile : (head + 1) * tile]
 
     @pl.loop(0, count // tile)
     def _(index):
@@ -367,9 +443,9 @@
             pl.when(cond)(functools.partial(run, index, blocks))
 
 
-def attend(queries, keys, values, segs, prefix):
+def attend(queries, span, segs, prefix):
     blocks, count, width = queries.shape
-    kv_heads = keys.shape[2] // HEAD_DIM
+    kv_heads = span.shape[2] // HEAD_DIM // 2
     group = width // kv_heads
     tile = 128
     starts = segs[:, ::tile]
@@ -382,8 +458,8 @@
         in_specs=[
             smem, smem,
             pl.BlockSpec((1, count, group), lambda b, h: (b, 0, h)),
-            pl.BlockSpec((keys.shape[0], count, HEAD_DIM), lambda b, h: (0, 0, h)),
-            pl.BlockSpec((keys.shape[0], count, HEAD_DIM), lambda b, h: (0, 0, h)),
+            pl.BlockSpec((span.shape[0], count, HEAD_DIM), lambda b, h: (0, 0, h)),
+            pl.BlockSpec((span.shape[0], count, HEAD_DIM), lambda b, h: (0, 0, kv_heads + h)),
             pl.BlockSpec((1, count, 1), lambda b, h: (b, 0, 0)),
             pl.BlockSpec((1, 1, count), lambda b, h: (b, 0, 0)),
         ],
@@ -392,31 +468,24 @@
         cost_estimate=pl.CostEstimate(
             flops=4 * blocks * count * width * count * (REACH + 1),
             bytes_accessed=8 * blocks * count * width, transcendentals=0),
-    )(reach, prefix, queries, keys, values, segs[:, :, None], segs[:, None, :])
+    )(reach, prefix, queries, span, span, segs[:, :, None], segs[:, None, :])
 
 
 def on_device(tokens, qkv_weight, segments, destination, doc_prefix):
     n_seq = lax.axis_size("seq")
     me = lax.axis_index("seq")
     count = tokens.shape[1]
-    meta = jnp.zeros((META_ROWS, count), jnp.int32)
-    meta = meta.at[0].set(segments[0]).at[1].set(destination[0]).at[2].set(doc_prefix[0, 0])
+    prefix_row = jnp.broadcast_to(doc_prefix[0], (count,))
+    meta = jnp.stack([segments[0], destination[0]] + [prefix_row] * (META_ROWS - 2))
+    turn = turns(segments[0], doc_prefix[0, 0])
     planar = n_seq == 4 * CORES
-    projected, metas = (project if planar else project_plain)(tokens[0], qkv_weight, meta)
+    queries, span, metas = (project if planar else project_plain)(
+        tokens[0], qkv_weight, meta, turn)
 
     pair = lax.dynamic_slice_in_dim(metas, me // CORES * CORES, CORES, 0)
-    segs, prefix = pair[:, 0], pair[:, 2, 0]
-    targets = pair[:, 1]
-    heads_per = HEADS // CORES * HEAD_DIM
-    kv_per = KV_HEADS // CORES * HEAD_DIM
-    position = jax.vmap(positions)(segs, prefix).reshape(-1)
-    keys = rotate(projected[:, heads_per : heads_per + kv_per], position)
-    values = projected[:, heads_per + kv_per :].astype(jnp.bfloat16)
-    own = jnp.concatenate([keys, values], axis=1)
-    before = lax.ppermute(own, "seq", [(i, i + CORES) for i in range(n_seq - CORES)])
-    queries = rotate(projected[:, :heads_per], position).reshape(CORES, count, heads_per)
-    span = jnp.concatenate([before, own]).reshape(2 * CORES, count, 2 * kv_per)
-    heads_out = attend(queries, span[:, :, :kv_per], span[:, :, kv_per:], segs, prefix)
+    segs, targets, prefix = pair[:, 0], pair[:, 1], pair[:, 2, 0]
+    heads_per = queries.shape[2]
+    heads_out = attend(queries, span, segs, prefix)
 
     capacity = count // min(n_seq, 16)
     slots = jnp.arange(n_seq * capacity, dtype=jnp.int32)

time: 201 us -> 195 us (0.970)
  Pallas kernels: 134 us -> 146 us
  local copies, waits for them, and re-layouts: 18 us -> 8.99 us
  starting transfers between devices: 8.11 us -> 4.04 us
  other arithmetic: 16.6 us -> 12.7 us
    pallas_call x1, Pallas kernels: 113 us -> 136 us  [project(): pl.pallas_call(functools.partial(project_kernel, depth, n_seq), out_shape...]
    pallas_call x1, Pallas kernels: 21.7 us -> 9.75 us  [attend(): pl.pallas_call(functools.partial(attend_kernel, tile), grid=(blocks, kv_h...]
    unnamed x12 -> x7, local copies, waits for them, and re-layouts: 11.5 us -> 2.84 us
    concatenate x4 -> x1, other arithmetic: 5.31 us -> 0.97 us  [turns(): return jnp.concatenate([cosine, cosine, -sine, sine], axis=1)]
    ppermute x1 -> x0, starting transfers between devices: 4.23 us -> none  [on_device(): lax.ppermute(own, 'seq', [(i, i + CORES) for i in range(n_seq - CORES)])]
    another operation x11 -> x6, other arithmetic: 6.34 us -> 2.72 us
    slice x5 -> x4, local copies, waits for them, and re-layouts: 0.38 us -> 3.04 us  [the longest x2 1.57 us: on_device(): segs, targets, prefix = (pair[:, 0], pair[:, 1], pair[:, 2, 0])]
    convert_element_type x1 -> x0, local copies, waits for them, and re-layouts: 2.55 us -> none  [rotate(): return turned.reshape(rows, width).astype(jnp.bfloat16)]
  transfers between devices with their start and end apart: 2 -> 1, of which waited for: 1 -> 1; matrix products, arithmetic and copies ran while one was open for 9% -> 2% of each run, Pallas kernels for 0% -> 0%
where the time goes in v2:
time: 195 us; the launch traced here: 192 us
  Pallas kernels  146 us (75%)
  waiting for transfers between devices  17.5 us (9%)
  other arithmetic  12.7 us (7%)
  local copies, waits for them, and re-layouts  8.99 us (5%)
  starting transfers between devices  4.04 us (2%)
  matrix products  2.31 us (1%)
    pallas_call x1, Pallas kernels, project(): pl.pallas_call(functools.partial(project_kernel, depth, n_seq), out_shape...  136 us
    all_to_all x1, waiting for transfers between devices, on_device(): lax.all_to_all(send_rows, 'seq', split_axis=0, concat_axis=0, tiled=True)  17.5 us
    pallas_call x1, Pallas kernels, attend(): pl.pallas_call(functools.partial(attend_kernel, tile), grid=(blocks, kv_h...  9.75 us
    all_to_all x1, starting transfers between devices, on_device(): lax.all_to_all(send_rows, 'seq', split_axis=0, concat_axis=0, tiled=True)  4.04 us
  transfers between devices with their start and end apart: 1, of which 1 were waited for; matrix products, arithmetic and copies ran while one was open for 2% of the time, Pallas kernels for 0%

profile of v2, /device:TPU:0, one launch (start us, length us, event | category | flops | bytes accessed | tf_op | source)
XLA Modules:
  0.0 192.1 jit_solution(17576494644041892388)
XLA Ops:
  0.0 1.2 slice.60
  1.3 0.7 reduce
  2.6 0.2 convert_reduce_fusion
  2.9 1.3 stack.6.meta_ref
  4.2 0.7 add_convert_fusion
  4.9 0.8 multiply_cosine_fusion
  5.6 1.0 pad_maximum_fusion.1.turn_ref
  6.6 135.9 %shard_map.55 = (bf16[2,384,1024]{2,1,0:T(8,128)(2,1)}, bf16[4,384,512]{2,1,0:T(8,128)(2,1)}, s32[8,8,384]{2,1,0:T(8,128)}) custom-call(bf16[384,4096]{1,0:T(8,128)(2,1)} %bitcast.78, bf16[128,3072]{1,0:T(8,128)(2,1)} %w_ref.1, s32[8,384]{1,0:T(8,128)} %stack.6.meta_ref, f32[384,256]{1,0:T(8,128)} %pad_maximum_fusion.1.turn_ref), custom_call_target="tpu_custom_call" | custom-call | flops 9663676416 | bytes 25165824 | tf_op jit(solution)/shard_map/pallas_call | solution.py:318
  142.6 0.7 constant_dynamic-slice_fusion.row_ref
  143.3 0.1 slice_reduce_fusion.3
  143.4 0.1 slice.68
  143.5 0.7 fusion.17
  144.3 0.8 and_reduce_fusion.1
  145.0 0.8 divide_reduce_fusion.1
  145.8 0.8 dynamic-slice_reduce_fusion.prefix_ref
  146.7 0.9 reduce-window.26
  147.5 0.2 slice_reduce_fusion
  147.8 0.1 fusion.9
  147.9 0.9 reduce-window.24
  148.8 0.2 slice_reduce_fusion.1
  149.0 0.1 fusion.10
  149.1 0.2 copy.26.col_ref
  149.3 0.1 compare_select_fusion.reach_ref
  149.4 0.0 copy-start
  149.4 1.4 copy-done
  150.8 0.0 copy-start.1
  150.8 1.4 copy-done.1
  152.2 9.8 %shard_map.56 = bf16[2,384,1024]{2,1,0:T(8,128)(2,1)S(1)} custom-call(s32[2,3]{1,0:T(2,128)S(1)} %compare_select_fusion.reach_ref, s32[2]{0:T(128)S(1)} %dynamic-slice_reduce_fusion.prefix_ref, bf16[2,384,1024]{2,1,0:T(8,128)(2,1)S(1)} %copy-done, bf16[4,384,512]{2,1,0:T(8,128)(2,1)S(1)} %copy-done.1, bf16[4,384,512]{2,1,0:T(8,128)(2,1)S(1)} %copy-done.1, ...), custom_call_target="tpu_custom_call" | custom-call | flops 3623878656 | bytes 6291456 | tf_op jit(solution)/shard_map/pallas_call | solution.py:454
  162.0 0.6 convolution_convert_fusion.2
  162.6 0.6 convolution_convert_fusion.3
  163.1 1.3 pad_maximum_fusion
  164.4 4.0 %all-to-all-start = ((bf16[8,2,48,1024]{3,2,1,0:T(8,128)(2,1)}), bf16[8,2,48,1024]{3,2,1,0:T(8,128)(2,1)S(1)}, u32[]{:S(2)}, u32[]{:S(2)}) async-start(bf16[8,2,48,1024]{3,2,1,0:T(8,128)(2,1)} %pad_maximum_fusion), calls=%async_computation | async-start | bytes 3145728 | tf_op jit(solution)/shard_map/all_to_all | solution.py:503
  168.5 1.0 fusion.6
  169.5 1.0 fusion.8
  170.5 0.9 reduce-window.20
  171.3 0.2 slice_reduce_fusion.2
  171.6 0.1 add_bitcast_fusion
  171.7 0.2 select_reduce_fusion
  171.9 0.1 sub.57
  172.0 17.5 %all-to-all-done = bf16[8,2,48,1024]{3,2,1,0:T(8,128)(2,1)S(1)} async-done(((bf16[8,2,48,1024]{3,2,1,0:T(8,128)(2,1)}), bf16[8,2,48,1024]{3,2,1,0:T(8,128)(2,1)S(1)}, u32[]{:S(2)}, u32[]{:S(2)}) %all-to-all-start) | async-done | bytes 1572896 | tf_op jit(solution)/shard_map/all_to_all | solution.py:503
  189.5 0.2 fusion.14
  189.7 0.6 convolution_convert_fusion.1
  190.2 0.6 convolution_convert_fusion
  190.8 1.2 maximum_bitcast_fusion
  (16 shorter events, 0.2 us)
Async XLA Ops:
  149.4 1.4 copy-start
  150.8 1.4 copy-start.1
  164.4 25.1 %all-to-all-start = ((bf16[8,2,48,1024]{3,2,1,0:T(8,128)(2,1)}), bf16[8,2,48,1024]{3,2,1,0:T(8,128)(2,1)S(1)}, u32[]{:S(2)}, u32[]{:S(2)}) async-start(bf16[8,2,48,1024]{3,2,1,0:T(8,128)(2,1)} %pad_maximum_fusion), calls=%async_computation | async-start | bytes 3145728 | tf_op jit(solution)/shard_map/all_to_all | solution.py:503

commit v3 on v2

--- a/solution.py
+++ b/solution.py
@@ -18,7 +18,9 @@
 META_ROWS = 8
 
 ORDERS = ("zxy", "zyx", "xyz")
-HEAD_START = (2.5, 0, 0)
+BASES = (-1.5, -2.0, -2.5)
+HOP_COSTS = ((4.25, 3.75, 0.75), (4.75, 4.25, 0.75), (3.75, 2.25, 3.0))
+OPENING = ((8.0, -5.5, 6.0), (4.0, 2.0, -11.0), (-1.5, 0.0, 11.5))
 
 
 def part_bounds(width):
@@ -155,7 +157,7 @@
         pending.append((part, offset, hop))
 
     opening = [(part, hop) for part in range(3) for hop in forwards(ORDERS[part], (0, 0, 0), depth)]
-    opening.sort(key=lambda item: ORDERS[item[0]].index(item[1][0]))
+    opening.sort(key=lambda item: OPENING[item[0]]["xyz".index(item[1][0])])
     for part, hop in opening:
         start(part, (0, 0, 0), hop)
     tok_send.start()
@@ -202,9 +204,8 @@
 
     def rank(event):
         part, offset = event
-        hops = sum(abs(v) for v in offset)
-        last = max(ORDERS[part].index(a) for a, v in zip("xyz", offset) if v)
-        return (hops - HEAD_START[part], last, part)
+        cost = sum(abs(v) * c for v, c in zip(offset, HOP_COSTS[part]))
+        return (BASES[part] + cost, part, offset)
 
     events.sort(key=rank)
     lag = 6
@@ -261,11 +262,13 @@
         for hop in forwards(ORDERS[part], offset, depth):
             start(part, offset, hop)
         waiting.append((part, offset))
-        if len(waiting) > lag:
-            if not ready:
-                begin_products()
-                ready = True
-            use(waiting.pop(0))
+        if len(waiting) > lag and not ready:
+            begin_products()
+            ready = True
+        if ready:
+            for item in waiting[:2]:
+                use(item)
+            del waiting[:2]
     if not ready:
         begin_products()
     for item in waiting:
@@ -397,11 +400,12 @@
     return jnp.concatenate([cosine, cosine, -sine, sine], axis=1)
 
 
-def attend_kernel(tile, reach_ref, prefix_ref, q_ref, k_ref, v_ref, col_ref, row_ref, out_ref):
+def attend_kernel(tile, metas_ref, pair_ref, q_ref, k_ref, v_ref, out_ref):
     block = pl.program_id(0)
+    owner = lax.axis_index("seq") // CORES * CORES + block
     count = q_ref.shape[1]
     group = q_ref.shape[2] // HEAD_DIM
-    prefix = prefix_ref[block]
+    prefix = metas_ref[owner, 2, 0]
     factor = HEAD_DIM ** -0.5 * 1.4426950408889634
 
     def run(index, remote):
@@ -410,13 +414,14 @@
         window = pl.ds(block + REACH - remote, blocks)
         keys = k_ref[window].reshape(blocks * count, HEAD_DIM)
         values = v_ref[window].reshape(blocks * count, HEAD_DIM)
-        ids = col_ref[0, at, :]
+        row = pair_ref[owner, pl.ds(0, 1), :]
         columns = lax.broadcasted_iota(jnp.int32, (tile, count), 1)
         lines = lax.broadcasted_iota(jnp.int32, (tile, count), 0) + index * tile
-        seen = (columns <= lines) & (row_ref[0] == ids)
+        ids = jnp.sum(jnp.where(columns == lines, row, 0), axis=1, keepdims=True)
+        seen = (columns <= lines) & (row == ids)
         if remote:
             back = lax.broadcasted_iota(jnp.int32, (tile, remote * count), 1) - remote * count
-            lead = ids == row_ref[0][:, :1]
+            lead = ids == row[:, :1]
             seen = jnp.concatenate([(back >= -prefix) & lead, seen], axis=1)
         parts = [pl.ds(head * HEAD_DIM, HEAD_DIM) for head in range(group)]
         queries = jnp.concatenate([q_ref[0, at, cols] for cols in parts], axis=0)
@@ -435,7 +440,8 @@
 
     @pl.loop(0, count // tile)
     def _(index):
-        remote = reach_ref[block, index]
+        lead = metas_ref[owner, 0, index * tile] == metas_ref[owner, 0, 0]
+        remote = jnp.where(lead, prefix, 0)
         for blocks in range(REACH + 1):
             low = remote > (blocks - 1) * count
             high = remote <= blocks * count
@@ -443,73 +449,65 @@
             pl.when(cond)(functools.partial(run, index, blocks))
 
 
-def attend(queries, span, segs, prefix):
+def attend(queries, span, metas):
     blocks, count, width = queries.shape
     kv_heads = span.shape[2] // HEAD_DIM // 2
     group = width // kv_heads
     tile = 128
-    starts = segs[:, ::tile]
-    reach = jnp.where(starts == segs[:, :1], prefix[:, None], 0)
-    smem = pl.BlockSpec(memory_space=pltpu.SMEM)
     return pl.pallas_call(
         functools.partial(attend_kernel, tile),
         grid=(blocks, kv_heads),
         out_shape=jax.ShapeDtypeStruct(queries.shape, jnp.bfloat16),
         in_specs=[
-            smem, smem,
+            pl.BlockSpec(memory_space=pltpu.SMEM), pl.BlockSpec(memory_space=pltpu.VMEM),
             pl.BlockSpec((1, count, group), lambda b, h: (b, 0, h)),
             pl.BlockSpec((span.shape[0], count, HEAD_DIM), lambda b, h: (0, 0, h)),
             pl.BlockSpec((span.shape[0], count, HEAD_DIM), lambda b, h: (0, 0, kv_heads + h)),
-            pl.BlockSpec((1, count, 1), lambda b, h: (b, 0, 0)),
-            pl.BlockSpec((1, 1, count), lambda b, h: (b, 0, 0)),
         ],
         out_specs=pl.BlockSpec((1, count, group), lambda b, h: (b, 0, h)),
-        compiler_params=pltpu.CompilerParams(vmem_limit_bytes=32 * 2**20),
+        compiler_params=pltpu.CompilerParams(vmem_limit_bytes=60 * 2**20),
         cost_estimate=pl.CostEstimate(
             flops=4 * blocks * count * width * count * (REACH + 1),
             bytes_accessed=8 * blocks * count * width, transcendentals=0),
-    )(reach, prefix, queries, span, span, segs[:, :, None], segs[:, None, :])
+    )(metas, metas, queries, span, span)
 
 
 def on_device(tokens, qkv_weight, segments, destination, doc_prefix):
     n_seq = lax.axis_size("seq")
     me = lax.axis_index("seq")
     count = tokens.shape[1]
+    capacity = count // min(n_seq, 16)
+    target = destination[0]
+    owner = lax.div(target, count)
+    index_list = jnp.arange(count, dtype=jnp.int32)
+    earlier = (owner[None, :] == owner[:, None]) & (index_list[None, :] < index_list[:, None])
+    core = lax.rem(me, CORES)
+    slot = (owner * CORES + core) * capacity + jnp.sum(earlier.astype(jnp.int32), axis=1)
     prefix_row = jnp.broadcast_to(doc_prefix[0], (count,))
-    meta = jnp.stack([segments[0], destination[0]] + [prefix_row] * (META_ROWS - 2))
+    meta = jnp.stack([segments[0], target, prefix_row, slot] + [slot] * (META_ROWS - 4))
     turn = turns(segments[0], doc_prefix[0, 0])
     planar = n_seq == 4 * CORES
     queries, span, metas = (project if planar else project_plain)(
         tokens[0], qkv_weight, meta, turn)
-
-    pair = lax.dynamic_slice_in_dim(metas, me // CORES * CORES, CORES, 0)
-    segs, targets, prefix = pair[:, 0], pair[:, 1], pair[:, 2, 0]
     heads_per = queries.shape[2]
-    heads_out = attend(queries, span, segs, prefix)
-
-    capacity = count // min(n_seq, 16)
-    slots = jnp.arange(n_seq * capacity, dtype=jnp.int32)
-
-    def pick(target, rows):
-        owner = target // count
-        one_hot = (owner[:, None] == jnp.arange(n_seq, dtype=jnp.int32)[None, :]).astype(jnp.int32)
-        order = jnp.sum(jnp.cumsum(one_hot, axis=0) * one_hot, axis=1) - 1
-        chosen = (slots[:, None] == (owner * capacity + order)[None, :]).astype(jnp.bfloat16)
-        return jnp.dot(chosen, rows, preferred_element_type=jnp.float32).astype(jnp.bfloat16)
-
-    send_rows = jnp.stack(
-        [pick(targets[j], heads_out[j]).reshape(n_seq, capacity, heads_per) for j in range(CORES)],
-        axis=1)
-    got = lax.all_to_all(send_rows, "seq", split_axis=0, concat_axis=0, tiled=True)
+    heads_out = attend(queries, span, metas)
+
+    slots = jnp.arange(n_seq * CORES * capacity, dtype=jnp.int32)
+    pair_slots = lax.dynamic_slice_in_dim(metas[:, 3], me - core, CORES, 0).reshape(1, -1)
+    chosen = (slots[:, None] == pair_slots).astype(jnp.bfloat16)
+    send_rows = jnp.dot(chosen, heads_out.reshape(CORES * count, heads_per),
+                        preferred_element_type=jnp.float32).astype(jnp.bfloat16)
+    got = lax.all_to_all(send_rows.reshape(n_seq, CORES * capacity, heads_per), "seq",
+                         split_axis=0, concat_axis=0, tiled=True)
     got = got.reshape(n_seq // CORES, CORES, CORES, capacity, heads_per)
 
-    everyone = metas[:, 1]
-    ours = everyone // count == me
-    order = jnp.cumsum(ours.astype(jnp.int32), axis=1) - 1
-    match = ours[:, None, :] & (
-        order[:, None, :] == jnp.arange(capacity, dtype=jnp.int32)[None, :, None])
-    places = jnp.sum(jnp.where(match, everyone[:, None, :] % count + 1, 0), axis=2) - 1
-    put = (jnp.arange(count, dtype=jnp.int32)[:, None] == places.reshape(1, -1)).astype(jnp.bfloat16)
+    wanted = slots.reshape(n_seq, CORES, capacity)[0] + me * CORES * capacity
+    wanted = jnp.tile(wanted, (n_seq // CORES, 1))
+    match = metas[:, 3][:, None, :] == wanted[:, :, None]
+    places = jnp.sum(
+        jnp.where(match, lax.rem(metas[:, 1], count)[:, None, :] + 1, 0), axis=2) - 1
+    places = places.reshape(-1)
+    put = (index_list[:, None] == places[None, :]).astype(jnp.bfloat16)
     halves = [
         jnp.dot(put, got[:, c].reshape(n_seq * capacity, heads_per),
                 preferred_element_type=jnp.float32).astype(jnp.bfloat16)

time: 195 us -> 177 us (0.908)
  the two profiles are of different devices: /device:TPU:0 before, /device:TPU:8 now
where the time goes in v3:
time: 177 us
  Pallas kernels  124 us (70%)
  waiting for transfers between devices  20.6 us (12%)
  starting transfers between devices  16.1 us (9%)
  other arithmetic  6.91 us (4%)
  matrix products  5.1 us (3%)
  local copies, waits for them, and re-layouts  2.83 us (2%)
    pallas_call x1, Pallas kernels, project(): pl.pallas_call(functools.partial(project_kernel, depth, n_seq), out_shape...  112 us
    all_to_all x1, waiting for transfers between devices, on_device(): lax.all_to_all(send_rows.reshape(n_seq, CORES * capacity, heads_per), 'se...  20.6 us
    all_to_all x1, starting transfers between devices, on_device(): lax.all_to_all(send_rows.reshape(n_seq, CORES * capacity, heads_per), 'se...  16.1 us
    pallas_call x1, Pallas kernels, attend(): pl.pallas_call(functools.partial(attend_kernel, tile), grid=(blocks, kv_h...  12 us
    dot_general x1, matrix products, on_device(): jnp.dot(chosen, heads_out.reshape(CORES * count, heads_per), preferred_el...  3.95 us
  transfers between devices with their start and end apart: 1, of which 1 were waited for; matrix products, arithmetic and copies ran while one was open for 0% of the time, Pallas kernels for 0%

profile of v3, /device:TPU:8, one launch (start us, length us, event | category | flops | bytes accessed | tf_op | source)
XLA Modules:
  0.0 176.7 jit_solution(1340676137326558395)
XLA Ops:
  0.0 0.7 reduce.1
  0.7 1.2 slice.20
  2.6 0.7 fusion.10
  3.3 0.2 convert_reduce_fusion.1
  3.5 0.2 convert_reduce_fusion
  3.8 1.3 stack.2.meta_ref
  5.1 0.7 add_convert_fusion
  5.8 0.8 multiply_cosine_fusion
  6.6 1.0 pad_maximum_fusion.turn_ref
  7.6 112.5 %shard_map.55 = (bf16[2,384,1024]{2,1,0:T(8,128)(2,1)}, bf16[4,384,512]{2,1,0:T(8,128)(2,1)}, s32[8,8,384]{2,1,0:T(8,128)}) custom-call(bf16[384,4096]{1,0:T(8,128)(2,1)} %bitcast.26, bf16[128,3072]{1,0:T(8,128)(2,1)} %w_ref.1, s32[8,384]{1,0:T(8,128)} %stack.2.meta_ref, f32[384,256]{1,0:T(8,128)} %pad_maximum_fusion.turn_ref), custom_call_target="tpu_custom_call" | custom-call | flops 9663676416 | bytes 25165824 | tf_op jit(solution)/shard_map/pallas_call | solution.py:321
  120.0 1.0 remainder_add_fusion
  121.1 12.0 %shard_map.56 = bf16[2,384,1024]{2,1,0:T(8,128)(2,1)} custom-call(s32[8,8,384]{2,1,0:T(8,128)} %get-tuple-element.8.metas_ref.pair_ref, s32[8,8,384]{2,1,0:T(8,128)} %get-tuple-element.8.metas_ref.pair_ref, bf16[2,384,1024]{2,1,0:T(8,128)(2,1)} %get-tuple-element.9.q_ref, bf16[4,384,512]{2,1,0:T(8,128)(2,1)} %get-tuple-element.10.k_ref.v_ref, ...), custom_call_target="tpu_custom_call" | custom-call | flops 3623878656 | bytes 6291456 | tf_op jit(solution)/shard_map/pallas_call | solution.py:457
  133.1 3.9 %fusion.1 = bf16[768,1024]{1,0:T(8,128)(2,1)} fusion(bf16[768,1024]{1,0:T(8,128)(2,1)} %bitcast.27, s32[768]{0:T(1024)S(1)} %eq.85), kind=kOutput, calls=%fused_computation.2 | convolution fusion | flops 1209335808 | bytes 3148800 | tf_op jit(solution)/shard_map/dot_general | solution.py:498
  137.0 16.1 %all-to-all-start = ((bf16[8,96,1024]{2,1,0:T(8,128)(2,1)}), bf16[8,96,1024]{2,1,0:T(8,128)(2,1)S(1)}, u32[]{:S(2)}, u32[]{:S(2)}) async-start(bf16[8,96,1024]{2,1,0:T(8,128)(2,1)} %bitcast.6), calls=%async_computation | async-start | bytes 3145728 | tf_op jit(solution)/shard_map/all_to_all | solution.py:500
  153.2 0.3 select_reduce_fusion
  153.5 0.1 sub.18
  153.6 20.6 %all-to-all-done = bf16[8,96,1024]{2,1,0:T(8,128)(2,1)S(1)} async-done(((bf16[8,96,1024]{2,1,0:T(8,128)(2,1)}), bf16[8,96,1024]{2,1,0:T(8,128)(2,1)S(1)}, u32[]{:S(2)}, u32[]{:S(2)}) %all-to-all-start) | async-done | bytes 1572896 | tf_op jit(solution)/shard_map/all_to_all | solution.py:500
  174.2 0.2 fusion.11
  174.3 0.6 convolution_convert_fusion
  174.9 0.6 convolution_convert_fusion.1
  175.5 1.2 maximum_bitcast_fusion
  (9 shorter events, 0.1 us)
Async XLA Ops:
  137.0 37.1 %all-to-all-start = ((bf16[8,96,1024]{2,1,0:T(8,128)(2,1)}), bf16[8,96,1024]{2,1,0:T(8,128)(2,1)S(1)}, u32[]{:S(2)}, u32[]{:S(2)}) async-start(bf16[8,96,1024]{2,1,0:T(8,128)(2,1)} %bitcast.6), calls=%async_computation | async-start | bytes 3145728 | tf_op jit(solution)/shard_map/all_to_all | solution.py:500

commit v4 on v3

--- a/solution.py
+++ b/solution.py
@@ -400,7 +400,7 @@
     return jnp.concatenate([cosine, cosine, -sine, sine], axis=1)
 
 
-def attend_kernel(tile, metas_ref, pair_ref, q_ref, k_ref, v_ref, out_ref):
+def attend_kernel(tile, metas_ref, pair_ref, q_ref, k_ref, v_ref, out_ref, rows_ref):
     block = pl.program_id(0)
     owner = lax.axis_index("seq") // CORES * CORES + block
     count = q_ref.shape[1]
@@ -432,11 +432,11 @@
         top = jnp.max(scores, axis=-1, keepdims=True)
         expo = jnp.exp2((scores - top) * factor)
         total = jnp.sum(expo, axis=-1, keepdims=True)
-        probs = (expo * (1.0 / total)).astype(jnp.bfloat16)
-        out = jnp.dot(probs.reshape(group * tile, blocks * count), values,
-                      preferred_element_type=jnp.float32).astype(jnp.bfloat16)
+        out = jnp.dot(expo.astype(jnp.bfloat16).reshape(group * tile, blocks * count), values,
+                      preferred_element_type=jnp.float32)
+        out = (out.reshape(group, tile, HEAD_DIM) * (1.0 / total)).astype(jnp.bfloat16)
         for head, cols in enumerate(parts):
-            out_ref[0, at, cols] = out[head * tile : (head + 1) * tile]
+            rows_ref[at, cols] = out[head]
 
     @pl.loop(0, count // tile)
     def _(index):
@@ -449,26 +449,35 @@
             pl.when(cond)(functools.partial(run, index, blocks))
 
 
-def attend(queries, span, metas):
+    devices, _, capacity, width = out_ref.shape
+    key = lax.broadcasted_iota(jnp.int32, (devices * capacity, count), 0)
+    key = key // capacity * (CORES * capacity) + block * capacity + key % capacity
+    chosen = jnp.where(key == pair_ref[owner, pl.ds(3, 1), :], 1.0, 0.0).astype(jnp.bfloat16)
+    sent = jnp.dot(chosen, rows_ref[...], preferred_element_type=jnp.float32)
+    out_ref[...] = sent.reshape(devices, 1, capacity, width).astype(jnp.bfloat16)
+
+
+def attend(head, capacity, queries, span, metas):
     blocks, count, width = queries.shape
+    n_seq = metas.shape[0]
     kv_heads = span.shape[2] // HEAD_DIM // 2
     group = width // kv_heads
-    tile = 128
     return pl.pallas_call(
-        functools.partial(attend_kernel, tile),
-        grid=(blocks, kv_heads),
-        out_shape=jax.ShapeDtypeStruct(queries.shape, jnp.bfloat16),
+        functools.partial(attend_kernel, 128),
+        grid=(blocks,),
+        out_shape=jax.ShapeDtypeStruct((n_seq, blocks, capacity, group), jnp.bfloat16),
         in_specs=[
             pl.BlockSpec(memory_space=pltpu.SMEM), pl.BlockSpec(memory_space=pltpu.VMEM),
-            pl.BlockSpec((1, count, group), lambda b, h: (b, 0, h)),
-            pl.BlockSpec((span.shape[0], count, HEAD_DIM), lambda b, h: (0, 0, h)),
-            pl.BlockSpec((span.shape[0], count, HEAD_DIM), lambda b, h: (0, 0, kv_heads + h)),
+            pl.BlockSpec((1, count, group), lambda b: (b, 0, head)),
+            pl.BlockSpec((span.shape[0], count, HEAD_DIM), lambda b: (0, 0, head)),
+            pl.BlockSpec((span.shape[0], count, HEAD_DIM), lambda b: (0, 0, kv_heads + head)),
         ],
-        out_specs=pl.BlockSpec((1, count, group), lambda b, h: (b, 0, h)),
+        out_specs=pl.BlockSpec((n_seq, 1, capacity, group), lambda b: (0, b, 0, 0)),
+        scratch_shapes=[pltpu.VMEM((count, group), jnp.bfloat16)],
         compiler_params=pltpu.CompilerParams(vmem_limit_bytes=60 * 2**20),
         cost_estimate=pl.CostEstimate(
-            flops=4 * blocks * count * width * count * (REACH + 1),
-            bytes_accessed=8 * blocks * count * width, transcendentals=0),
+            flops=4 * blocks * count * group * count * (REACH + 1),
+            bytes_accessed=8 * blocks * count * group, transcendentals=0),
     )(metas, metas, queries, span, span)
 
 
@@ -489,19 +498,17 @@
     planar = n_seq == 4 * CORES
     queries, span, metas = (project if planar else project_plain)(
         tokens[0], qkv_weight, meta, turn)
-    heads_per = queries.shape[2]
-    heads_out = attend(queries, span, metas)
-
-    slots = jnp.arange(n_seq * CORES * capacity, dtype=jnp.int32)
-    pair_slots = lax.dynamic_slice_in_dim(metas[:, 3], me - core, CORES, 0).reshape(1, -1)
-    chosen = (slots[:, None] == pair_slots).astype(jnp.bfloat16)
-    send_rows = jnp.dot(chosen, heads_out.reshape(CORES * count, heads_per),
-                        preferred_element_type=jnp.float32).astype(jnp.bfloat16)
-    got = lax.all_to_all(send_rows.reshape(n_seq, CORES * capacity, heads_per), "seq",
-                         split_axis=0, concat_axis=0, tiled=True)
-    got = got.reshape(n_seq // CORES, CORES, CORES, capacity, heads_per)
-
-    wanted = slots.reshape(n_seq, CORES, capacity)[0] + me * CORES * capacity
+    kv_heads = KV_HEADS // CORES
+    group = queries.shape[2] // kv_heads
+    got = []
+    for head in range(kv_heads):
+        sent = attend(head, capacity, queries, span, metas)
+        here = lax.all_to_all(sent.reshape(n_seq, CORES * capacity, group), "seq",
+                              split_axis=0, concat_axis=0, tiled=True)
+        got.append(here.reshape(n_seq // CORES, CORES, CORES, capacity, group))
+
+    wanted = jnp.arange(CORES * capacity, dtype=jnp.int32).reshape(CORES, capacity)
+    wanted = wanted + me * CORES * capacity
     wanted = jnp.tile(wanted, (n_seq // CORES, 1))
     match = metas[:, 3][:, None, :] == wanted[:, :, None]
     places = jnp.sum(
@@ -509,9 +516,10 @@
     places = places.reshape(-1)
     put = (index_list[:, None] == places[None, :]).astype(jnp.bfloat16)
     halves = [
-        jnp.dot(put, got[:, c].reshape(n_seq * capacity, heads_per),
+        jnp.dot(put, got[head][:, c].reshape(n_seq * capacity, group),
                 preferred_element_type=jnp.float32).astype(jnp.bfloat16)
         for c in range(CORES)
+        for head in range(kv_heads)
     ]
     return jnp.concatenate(halves, axis=1)[None]
 

time: 177 us -> 170 us (0.960); the launches traced: 177 us -> 167 us
  waiting for transfers between devices: 20.6 us -> 15.6 us
  matrix products: 5.1 us -> 1.5 us
  starting transfers between devices: 16.1 us -> 12.8 us
  Pallas kernels: 124 us -> 127 us
    all_to_all x1 -> x2, waiting for transfers between devices: 20.6 us -> 15.6 us  [on_device(): lax.all_to_all(sent.reshape(n_seq, CORES * capacity, group), 'seq', split...]
    dot_general x3 -> x4, matrix products: 5.1 us -> 1.5 us  [on_device(): jnp.dot(put, got[head][:, c].reshape(n_seq * capacity, group), preferred_...]
    all_to_all x1 -> x2, starting transfers between devices: 16.1 us -> 12.8 us  [on_device(): lax.all_to_all(sent.reshape(n_seq, CORES * capacity, group), 'seq', split...]
    pallas_call x1 -> x2, Pallas kernels: 12 us -> 14.6 us  [attend(): pl.pallas_call(functools.partial(attend_kernel, 128), grid=(blocks,), out...]
  transfers between devices with their start and end apart: 1 -> 2, of which waited for: 1 -> 2; matrix products, arithmetic and copies ran while one was open for 0% -> 1% of each run, Pallas kernels for 0% -> 4%
where the time goes in v4:
time: 170 us; the launch traced here: 167 us
  Pallas kernels  127 us (75%)
  waiting for transfers between devices  15.6 us (9%)
  starting transfers between devices  12.8 us (8%)
  other arithmetic  7.02 us (4%)
  local copies, waits for them, and re-layouts  2.79 us (2%)
    pallas_call x1, Pallas kernels, project(): pl.pallas_call(functools.partial(project_kernel, depth, n_seq), out_shape...  112 us
    all_to_all x2, waiting for transfers between devices, on_device(): lax.all_to_all(sent.reshape(n_seq, CORES * capacity, group), 'seq', split...  15.6 us
    pallas_call x2, Pallas kernels, attend(): pl.pallas_call(functools.partial(attend_kernel, 128), grid=(blocks,), out...  14.6 us
    all_to_all x2, starting transfers between devices, on_device(): lax.all_to_all(sent.reshape(n_seq, CORES * capacity, group), 'seq', split...  12.8 us
  transfers between devices with their start and end apart: 2, of which 2 were waited for; matrix products, arithmetic and copies ran while one was open for 1% of the time, Pallas kernels for 4%

profile of v4, /device:TPU:8, one launch (start us, length us, event | category | flops | bytes accessed | tf_op | source)
XLA Modules:
  0.0 167.5 jit_solution(2480496875241555312)
XLA Ops:
  0.0 1.2 slice.22
  1.3 0.7 reduce.1
  2.6 0.2 convert_reduce_fusion
  2.8 0.7 fusion.6
  3.5 0.2 convert_reduce_fusion.1
  3.8 1.3 stack.2.meta_ref
  5.1 0.7 add_convert_fusion
  5.8 0.8 multiply_cosine_fusion
  6.6 1.0 pad_maximum_fusion.turn_ref
  7.6 112.5 %shard_map.55 = (bf16[2,384,1024]{2,1,0:T(8,128)(2,1)}, bf16[4,384,512]{2,1,0:T(8,128)(2,1)}, s32[8,8,384]{2,1,0:T(8,128)}) custom-call(bf16[384,4096]{1,0:T(8,128)(2,1)} %bitcast.33, bf16[128,3072]{1,0:T(8,128)(2,1)} %w_ref.1, s32[8,384]{1,0:T(8,128)} %stack.2.meta_ref, f32[384,256]{1,0:T(8,128)} %pad_maximum_fusion.turn_ref), custom_call_target="tpu_custom_call" | custom-call | flops 9663676416 | bytes 25165824 | tf_op jit(solution)/shard_map/pallas_call | solution.py:321
  120.0 7.3 %shard_map.57 = bf16[8,2,48,512]{3,2,1,0:T(8,128)(2,1)} custom-call(s32[8,8,384]{2,1,0:T(8,128)} %get-tuple-element.8.metas_ref.pair_ref, s32[8,8,384]{2,1,0:T(8,128)} %get-tuple-element.8.metas_ref.pair_ref, bf16[2,384,1024]{2,1,0:T(8,128)(2,1)} %get-tuple-element.9.q_ref, bf16[4,384,512]{2,1,0:T(8,128)(2,1)} %get-tuple-element.10.k_ref.v_ref, ...), custom_call_target="tpu_custom_call" | custom-call | flops 1811939328 | bytes 3145728 | tf_op jit(solution)/shard_map/pallas_call | solution.py:465
  127.3 8.4 %all-to-all-start.1 = ((bf16[8,96,512]{2,1,0:T(8,128)(2,1)}), bf16[8,96,512]{2,1,0:T(8,128)(2,1)S(1)}, u32[]{:S(2)}, u32[]{:S(2)}) async-start(bf16[8,96,512]{2,1,0:T(8,128)(2,1)} %bitcast.26), calls=%async_computation.1 | async-start | bytes 1572864 | tf_op jit(solution)/shard_map/all_to_all | solution.py:506
  135.8 1.0 fusion.9
  136.8 0.3 select_reduce_fusion
  137.2 0.1 sub.15
  137.3 7.3 %shard_map.56 = bf16[8,2,48,512]{3,2,1,0:T(8,128)(2,1)} custom-call(s32[8,8,384]{2,1,0:T(8,128)} %get-tuple-element.8.metas_ref.pair_ref, s32[8,8,384]{2,1,0:T(8,128)} %get-tuple-element.8.metas_ref.pair_ref, bf16[2,384,1024]{2,1,0:T(8,128)(2,1)} %get-tuple-element.9.q_ref, bf16[4,384,512]{2,1,0:T(8,128)(2,1)} %get-tuple-element.10.k_ref.v_ref, ...), custom_call_target="tpu_custom_call" | custom-call | flops 1811939328 | bytes 3145728 | tf_op jit(solution)/shard_map/pallas_call | solution.py:465
  144.6 3.8 %all-to-all-done.1 = bf16[8,96,512]{2,1,0:T(8,128)(2,1)S(1)} async-done(((bf16[8,96,512]{2,1,0:T(8,128)(2,1)}), bf16[8,96,512]{2,1,0:T(8,128)(2,1)S(1)}, u32[]{:S(2)}, u32[]{:S(2)}) %all-to-all-start.1) | async-done | bytes 786464 | tf_op jit(solution)/shard_map/all_to_all | solution.py:506
  148.4 4.3 %all-to-all-start = ((bf16[8,96,512]{2,1,0:T(8,128)(2,1)}), bf16[8,96,512]{2,1,0:T(8,128)(2,1)S(1)}, u32[]{:S(2)}, u32[]{:S(2)}) async-start(bf16[8,96,512]{2,1,0:T(8,128)(2,1)} %bitcast.27), calls=%async_computation | async-start | bytes 1572864 | tf_op jit(solution)/shard_map/all_to_all | solution.py:506
  152.7 0.1 fusion.8
  152.8 0.4 convolution_convert_fusion.2
  153.2 0.4 convolution_convert_fusion
  153.5 11.8 %all-to-all-done = bf16[8,96,512]{2,1,0:T(8,128)(2,1)S(1)} async-done(((bf16[8,96,512]{2,1,0:T(8,128)(2,1)}), bf16[8,96,512]{2,1,0:T(8,128)(2,1)S(1)}, u32[]{:S(2)}, u32[]{:S(2)}) %all-to-all-start) | async-done | bytes 786464 | tf_op jit(solution)/shard_map/all_to_all | solution.py:506
  165.3 0.1 fusion.7
  165.4 0.4 convolution_convert_fusion.3
  165.8 0.4 convolution_convert_fusion.1
  166.1 1.4 maximum_bitcast_fusion
  (7 shorter events, 0.0 us)
Async XLA Ops:
  127.3 21.1 %all-to-all-start.1 = ((bf16[8,96,512]{2,1,0:T(8,128)(2,1)}), bf16[8,96,512]{2,1,0:T(8,128)(2,1)S(1)}, u32[]{:S(2)}, u32[]{:S(2)}) async-start(bf16[8,96,512]{2,1,0:T(8,128)(2,1)} %bitcast.26), calls=%async_computation.1 | async-start | bytes 1572864 | tf_op jit(solution)/shard_map/all_to_all | solution.py:506
  148.4 16.9 %all-to-all-start = ((bf16[8,96,512]{2,1,0:T(8,128)(2,1)}), bf16[8,96,512]{2,1,0:T(8,128)(2,1)S(1)}, u32[]{:S(2)}, u32[]{:S(2)}) async-start(bf16[8,96,512]{2,1,0:T(8,128)(2,1)} %bitcast.27), calls=%async_computation | async-start | bytes 1572864 | tf_op jit(solution)/shard_map/all_to_all | solution.py:506

commit v5 on v4

--- a/solution.py
+++ b/solution.py
@@ -391,7 +391,7 @@
     first_row = jnp.sum(
         (segment_ids[None, :] < segment_ids[:, None]).astype(jnp.int32), axis=1)
     index_list = jnp.arange(segment_ids.shape[0], dtype=jnp.int32)
-    leading = segment_ids == segment_ids[0]
+    leading = first_row == 0
     position = index_list - first_row + jnp.where(leading, prefix_len, 0)
     half_dim = HEAD_DIM // 2
     frequency = ROPE_BASE ** (-2.0 * jnp.arange(half_dim, dtype=jnp.float32) / HEAD_DIM)
@@ -463,7 +463,7 @@
     kv_heads = span.shape[2] // HEAD_DIM // 2
     group = width // kv_heads
     return pl.pallas_call(
-        functools.partial(attend_kernel, 128),
+        functools.partial(attend_kernel, count // 2),
         grid=(blocks,),
         out_shape=jax.ShapeDtypeStruct((n_seq, blocks, capacity, group), jnp.bfloat16),
         in_specs=[

time: 170 us -> 166 us (0.976)
  the two profiles are of different devices: /device:TPU:8 before, /device:TPU:0 now
where the time goes in v5:
time: 166 us
  Pallas kernels  128 us (77%)
  waiting for transfers between devices  15 us (9%)
  starting transfers between devices  13 us (8%)
  other arithmetic  6.33 us (4%)
    pallas_call x1, Pallas kernels, project(): pl.pallas_call(functools.partial(project_kernel, depth, n_seq), out_shape...  112 us
    pallas_call x2, Pallas kernels, attend(): pl.pallas_call(functools.partial(attend_kernel, count // 2), grid=(blocks...  15.8 us
    all_to_all x2, waiting for transfers between devices, on_device(): lax.all_to_all(sent.reshape(n_seq, CORES * capacity, group), 'seq', split...  15 us
    all_to_all x2, starting transfers between devices, on_device(): lax.all_to_all(sent.reshape(n_seq, CORES * capacity, group), 'seq', split...  13 us
  transfers between devices with their start and end apart: 2, of which 2 were waited for; matrix products, arithmetic and copies ran while one was open for 1% of the time, Pallas kernels for 5%

profile of v5, /device:TPU:0, one launch (start us, length us, event | category | flops | bytes accessed | tf_op | source)
XLA Modules:
  0.0 166.3 jit_solution(13436275031777695785)
XLA Ops:
  0.7 0.7 reduce.1
  1.4 0.2 convert_reduce_fusion
  1.6 0.7 fusion.6
  2.3 0.2 convert_reduce_fusion.1
  2.6 1.3 stack.2.meta_ref
  3.9 0.8 multiply_cosine_fusion
  4.7 1.0 pad_maximum_fusion.turn_ref
  5.6 112.4 %shard_map.55 = (bf16[2,384,1024]{2,1,0:T(8,128)(2,1)}, bf16[4,384,512]{2,1,0:T(8,128)(2,1)}, s32[8,8,384]{2,1,0:T(8,128)}) custom-call(bf16[384,4096]{1,0:T(8,128)(2,1)} %bitcast.32, bf16[128,3072]{1,0:T(8,128)(2,1)} %w_ref.1, s32[8,384]{1,0:T(8,128)} %stack.2.meta_ref, f32[384,256]{1,0:T(8,128)} %pad_maximum_fusion.turn_ref), custom_call_target="tpu_custom_call" | custom-call | flops 9663676416 | bytes 25165824 | tf_op jit(solution)/shard_map/pallas_call | solution.py:321
  118.0 7.9 %shard_map.57 = bf16[8,2,48,512]{3,2,1,0:T(8,128)(2,1)} custom-call(s32[8,8,384]{2,1,0:T(8,128)} %get-tuple-element.8.metas_ref.pair_ref, s32[8,8,384]{2,1,0:T(8,128)} %get-tuple-element.8.metas_ref.pair_ref, bf16[2,384,1024]{2,1,0:T(8,128)(2,1)} %get-tuple-element.9.q_ref, bf16[4,384,512]{2,1,0:T(8,128)(2,1)} %get-tuple-element.10.k_ref.v_ref, ...), custom_call_target="tpu_custom_call" | custom-call | flops 1811939328 | bytes 3145728 | tf_op jit(solution)/shard_map/pallas_call | solution.py:465
  126.0 8.3 %all-to-all-start.1 = ((bf16[8,96,512]{2,1,0:T(8,128)(2,1)}), bf16[8,96,512]{2,1,0:T(8,128)(2,1)S(1)}, u32[]{:S(2)}, u32[]{:S(2)}) async-start(bf16[8,96,512]{2,1,0:T(8,128)(2,1)} %bitcast.25), calls=%async_computation.1 | async-start | bytes 1572864 | tf_op jit(solution)/shard_map/all_to_all | solution.py:506
  134.2 1.0 fusion.9
  135.3 0.3 select_reduce_fusion
  135.6 0.1 sub.15
  135.7 7.9 %shard_map.56 = bf16[8,2,48,512]{3,2,1,0:T(8,128)(2,1)} custom-call(s32[8,8,384]{2,1,0:T(8,128)} %get-tuple-element.8.metas_ref.pair_ref, s32[8,8,384]{2,1,0:T(8,128)} %get-tuple-element.8.metas_ref.pair_ref, bf16[2,384,1024]{2,1,0:T(8,128)(2,1)} %get-tuple-element.9.q_ref, bf16[4,384,512]{2,1,0:T(8,128)(2,1)} %get-tuple-element.10.k_ref.v_ref, ...), custom_call_target="tpu_custom_call" | custom-call | flops 1811939328 | bytes 3145728 | tf_op jit(solution)/shard_map/pallas_call | solution.py:465
  143.6 3.2 %all-to-all-done.1 = bf16[8,96,512]{2,1,0:T(8,128)(2,1)S(1)} async-done(((bf16[8,96,512]{2,1,0:T(8,128)(2,1)}), bf16[8,96,512]{2,1,0:T(8,128)(2,1)S(1)}, u32[]{:S(2)}, u32[]{:S(2)}) %all-to-all-start.1) | async-done | bytes 786464 | tf_op jit(solution)/shard_map/all_to_all | solution.py:506
  146.8 4.7 %all-to-all-start = ((bf16[8,96,512]{2,1,0:T(8,128)(2,1)}), bf16[8,96,512]{2,1,0:T(8,128)(2,1)S(1)}, u32[]{:S(2)}, u32[]{:S(2)}) async-start(bf16[8,96,512]{2,1,0:T(8,128)(2,1)} %bitcast.26), calls=%async_computation | async-start | bytes 1572864 | tf_op jit(solution)/shard_map/all_to_all | solution.py:506
  151.5 0.1 fusion.8
  151.6 0.4 convolution_convert_fusion.2
  152.0 0.4 convolution_convert_fusion
  152.4 11.8 %all-to-all-done = bf16[8,96,512]{2,1,0:T(8,128)(2,1)S(1)} async-done(((bf16[8,96,512]{2,1,0:T(8,128)(2,1)}), bf16[8,96,512]{2,1,0:T(8,128)(2,1)S(1)}, u32[]{:S(2)}, u32[]{:S(2)}) %all-to-all-start) | async-done | bytes 786464 | tf_op jit(solution)/shard_map/all_to_all | solution.py:506
  164.1 0.1 fusion.7
  164.2 0.4 convolution_convert_fusion.3
  164.6 0.4 convolution_convert_fusion.1
  165.0 1.4 maximum_bitcast_fusion
  (8 shorter events, 0.0 us)
Async XLA Ops:
  126.0 20.9 %all-to-all-start.1 = ((bf16[8,96,512]{2,1,0:T(8,128)(2,1)}), bf16[8,96,512]{2,1,0:T(8,128)(2,1)S(1)}, u32[]{:S(2)}, u32[]{:S(2)}) async-start(bf16[8,96,512]{2,1,0:T(8,128)(2,1)} %bitcast.25), calls=%async_computation.1 | async-start | bytes 1572864 | tf_op jit(solution)/shard_map/all_to_all | solution.py:506
  146.8 17.3 %all-to-all-start = ((bf16[8,96,512]{2,1,0:T(8,128)(2,1)}), bf16[8,96,512]{2,1,0:T(8,128)(2,1)S(1)}, u32[]{:S(2)}, u32[]{:S(2)}) async-start(bf16[8,96,512]{2,1,0:T(8,128)(2,1)} %bitcast.26), calls=%async_computation | async-start | bytes 1572864 | tf_op jit(solution)/shard_map/all_to_all | solution.py:506
